TPU v7x, 32 devices: a whole 2x2x4 slice. The times are simulated.
32 devices in a mesh: grp: 2 (over x), section: 16 (over z, y, core).
Axes of the slice: x: 2, y: 2, z: 4, core: 2. Of those that a mesh axis runs over, the one named last changes fastest.
Arguments:
- latent: bfloat16 [1536, 64], P(('grp', 'section')), parts along dimension 0, may hold values from -6 to 6
- control_latent: bfloat16 [1536, 64], P(('grp', 'section')), parts along dimension 0, may hold values from -6 to 6
- patch_tiles: int32 [4], replicated, may hold values from 1 to 2, 6 in all
- tile_lists: int32 [2, 6, 3], replicated, may hold values from 0 to 5, as said below
- tile_counts: int32 [2, 6], replicated, may hold values from 1 to 3, as said below
- embed_weight: bfloat16 [64, 3072], replicated, may hold values from -0.75 to 0.75
- control_embed: bfloat16 [64, 3072], replicated, may hold values from -0.75 to 0.75
- modulation: float32 [2, 3, 3072], replicated, may hold values from -4 to 4
- qk_gain: float32 [2, 2, 128], replicated, may hold values from 0.1 to 1.9
- qkv_weight: bfloat16 [16, 3072, 1152], P('section'), may hold values from -0.109375 to 0.109375
- out_weight: bfloat16 [16, 384, 3072], P('section'), may hold values from -0.109375 to 0.109375
- stale_cache: bfloat16 [16, 1536, 768], P('section', 'grp'), parts along dimension 1, may hold values from -6 to 6
- control_gain: float32 [1, 3072], replicated, may hold values from -3 to 3
- final_mod: float32 [2, 3072], replicated, may hold values from -3 to 3
- final_weight: bfloat16 [3072, 64], replicated, may hold values from -0.109375 to 0.109375
Outputs:
- denoised: float32 [1536, 64], P(('grp', 'section')), parts along dimension 0
There are 2 independent parts, one for each index of `grp`. A program takes and returns all parts, laid end to end along the dimension named above; an argument that names none is the same for every part. Nothing has to cross between parts.
Inputs may be any that keep to these rules, and one draw needn't show every extreme that they name: `patch_tiles`: the patches are contiguous and in order and together cover all 6 tiles; the largest has exactly 2 tiles. Entry 0 of tile_lists[b, t] is t itself; the 3 entries of one row are distinct. `tile_counts`: in every block slot some query tile uses all 3 listed tiles.
All inputs are finite; a program needn't handle non-finite values.
Results may differ from a plain program's by a relative error of at most 0.014.
Values may be sent and summed in bfloat16 or wider, within the bound.
A program may use at most 64 MiB of HBM per device.

v0:
```python
import math

import jax
import jax.numpy as jnp
from jax import lax
from jax.sharding import PartitionSpec as P

D = 3072
HD = 128
HG = 8
C_OUT = 64
TILE = 128
KSEL = 3
PATCHES = 4
TILES = 6
PMAX = 2


EPSILON = 1e-06


def from_partner(value, axis, distance):
    return lax.ppermute(value, axis, [(i, i ^ 1 << distance) for i in range(lax.axis_size(axis))])


def from_behind(value, axis, steps):
    count = lax.axis_size(axis)
    leading, last = (max(0, -steps), min(count, count - steps))
    return lax.ppermute(value, axis, [(source, source + steps) for source in range(leading, last)])


def modulated(hidden, shift_row, scale_row):
    values = hidden.astype(jnp.float32)
    centered = values - jnp.mean(values, axis=-1, keepdims=True)
    variance = jnp.mean(centered * centered, axis=-1, keepdims=True)
    normed = centered * lax.rsqrt(variance + EPSILON)
    return (normed * (1.0 + scale_row) + shift_row).astype(jnp.bfloat16)


def rms_scaled(values, gain_row):
    return (
        values * lax.rsqrt(jnp.mean(values * values, axis=-1, keepdims=True) + EPSILON) * gain_row
    )


def attend_group(
    modded, w_qkv, w_out, memory, gain_pair, start_tile, patch_length, tile_list, tile_limit
):
    row_count = modded.shape[0]
    query_tiles_count = row_count // TILE
    head_count = w_out.shape[0] // HD
    projected = jnp.dot(modded, w_qkv, preferred_element_type=jnp.float32).reshape(
        row_count, 3, head_count, HD
    )
    queries = rms_scaled(projected[:, 0], gain_pair[0]).astype(jnp.bfloat16)
    keys_new = rms_scaled(projected[:, 1], gain_pair[1]).astype(jnp.bfloat16)
    values_new = projected[:, 2].astype(jnp.bfloat16)
    fresh_rows = jnp.concatenate(
        [
            keys_new.reshape(row_count, head_count * HD),
            values_new.reshape(row_count, head_count * HD),
        ],
        axis=1,
    )
    row_start = start_tile * TILE
    previous = lax.dynamic_slice_in_dim(memory, row_start, row_count, 0)
    live_rows = jnp.arange(row_count) < patch_length * TILE
    memory = lax.dynamic_update_slice_in_dim(
        memory, jnp.where(live_rows[:, None], fresh_rows, previous), row_start, 0
    )
    tiled_memory = memory.reshape(-1, TILE, 2, head_count, HD)
    query_tiles = jnp.minimum(start_tile + jnp.arange(query_tiles_count), TILES - 1)
    picked = tile_list[query_tiles]
    used_counts = tile_limit[query_tiles]
    chosen = tiled_memory[picked]
    key_rows = chosen[:, :, :, 0].reshape(query_tiles_count, KSEL * TILE, head_count, HD)
    value_rows = chosen[:, :, :, 1].reshape(query_tiles_count, KSEL * TILE, head_count, HD)
    query_rows = queries.reshape(query_tiles_count, TILE, head_count, HD)
    scores = jnp.einsum(
        "tqhd,tkhd->thqk", query_rows, key_rows, preferred_element_type=jnp.float32
    ) / math.sqrt(HD)
    allowed = (jnp.arange(KSEL * TILE) // TILE)[None, :] < used_counts[:, None]
    scores = jnp.where(allowed[:, None, None, :], scores, -1e30)
    highest = jnp.max(scores, axis=-1, keepdims=True)
    weights = jnp.exp(scores - highest)
    probabilities = (weights / jnp.sum(weights, axis=-1, keepdims=True)).astype(jnp.bfloat16)
    attended = jnp.einsum(
        "thqk,tkhd->tqhd", probabilities, value_rows, preferred_element_type=jnp.float32
    ).astype(jnp.bfloat16)
    attended = attended.reshape(row_count, head_count * HD)
    partial_value = jnp.dot(attended, w_out, preferred_element_type=jnp.float32)
    return (partial_value, memory)


def split_rows(current, upper_half):
    middle = current.shape[0] // 2
    kept = jnp.where(upper_half, current[middle:], current[:middle])
    given = jnp.where(upper_half, current[:middle], current[middle:])
    return (kept, given)


def on_device(
    latent,
    control_latent,
    patch_tiles,
    tile_lists,
    tile_counts,
    embed_weight,
    control_embed,
    modulation,
    qk_gain,
    qkv_weight,
    out_weight,
    stale_cache,
    control_gain,
    final_mod,
    final_weight,
):
    slot_count = lax.axis_size("section") // HG
    control_count = slot_count // 2
    device_index = lax.axis_index("section")
    slot_index = device_index // HG
    group_index = device_index % HG
    is_control = slot_index % 2 == 0
    chain_index = slot_index // 2
    row_count = PMAX * TILE
    share_rows = row_count // HG
    bit_count = HG.bit_length() - 1
    bit_order = list(range(bit_count - 1, -1, -1))
    share_start = jnp.zeros((), jnp.int32)
    for position, bit_index in enumerate(bit_order):
        share_start = share_start + (group_index >> bit_index & 1) * (row_count >> position + 1)
    whole_latent, whole_control = (
        lax.all_gather(latent, "section", axis=0, tiled=True),
        lax.all_gather(control_latent, "section", axis=0, tiled=True),
    )
    padding = ((0, row_count), (0, 0))
    latent_pad = jnp.pad(whole_latent, padding)
    control_pad = jnp.pad(whole_control, padding)
    seq_rows = whole_latent.shape[0]
    memory_start = jnp.pad(stale_cache[0], padding)
    w_qkv = qkv_weight[0]
    w_out = out_weight[0]
    shifts = modulation[slot_index]
    gain_pair = qk_gain[slot_index]
    tile_list = tile_lists[slot_index]
    tile_limit = tile_counts[slot_index]
    control_row = control_gain[jnp.minimum(chain_index, control_count - 1)]
    is_last_main = slot_index == slot_count - 1
    starts = jnp.cumsum(patch_tiles) - patch_tiles

    def reduce_share(partial_value):
        upper_half = group_index >> bit_order[0] & 1 == 1
        kept, given = split_rows(partial_value.astype(jnp.bfloat16), upper_half)
        summed = kept.astype(jnp.float32) + from_partner(given, "section", bit_order[0]).astype(
            jnp.float32
        )
        for bit_index in bit_order[1:]:
            upper_half = group_index >> bit_index & 1 == 1
            kept, given = split_rows(summed, upper_half)
            summed = kept + from_partner(given.astype(jnp.bfloat16), "section", bit_index).astype(
                given.dtype
            )
        return summed

    def gather_rows(gathered):
        for bit_index in reversed(bit_order):
            partner = from_partner(gathered, "section", bit_index)
            upper_half = group_index >> bit_index & 1 == 1
            gathered = jnp.where(
                upper_half,
                jnp.concatenate([partner, gathered]),
                jnp.concatenate([gathered, partner]),
            )
        return gathered

    def run_tick(tick_index, carry):
        inflow_hidden, inflow_control, memory, denoised = carry
        patch_index = tick_index - slot_index
        active = (patch_index >= 0) & (patch_index < PATCHES)
        patch_index = jnp.clip(patch_index, 0, PATCHES - 1)
        start_tile = starts[patch_index]
        patch_length = patch_tiles[patch_index]
        row_start = start_tile * TILE + share_start
        own_latent = lax.dynamic_slice_in_dim(latent_pad, row_start, share_rows, 0)
        own_control = lax.dynamic_slice_in_dim(control_pad, row_start, share_rows, 0)
        embedded = jnp.dot(own_latent, embed_weight, preferred_element_type=jnp.float32)
        conditioned = embedded + jnp.dot(
            own_control, control_embed, preferred_element_type=jnp.float32
        )
        first_slot = slot_index == 0
        current_hidden = jnp.where(first_slot, embedded.astype(jnp.bfloat16), inflow_hidden)
        current_control = jnp.where(first_slot, conditioned.astype(jnp.bfloat16), inflow_control)
        stream = jnp.where(is_control, current_control, current_hidden)
        gathered = gather_rows(stream)

        def compute(memory_in):
            modded = modulated(gathered, shifts[0], shifts[1])
            return attend_group(
                modded,
                w_qkv,
                w_out,
                memory_in,
                gain_pair,
                start_tile,
                patch_length,
                tile_list,
                tile_limit,
            )

        def skipped(memory_in):
            return (jnp.zeros((row_count, w_out.shape[1]), jnp.float32), memory_in)

        partial_value, memory = lax.cond(active, compute, skipped, memory)
        summed = reduce_share(partial_value)
        updated = stream.astype(jnp.float32) + shifts[2] * summed
        new_control = updated.astype(jnp.bfloat16)
        new_hidden = (updated + control_row * current_control.astype(jnp.float32)).astype(
            jnp.bfloat16
        )
        out_hidden = jnp.where(is_control, current_hidden, new_hidden)
        out_control = jnp.where(is_control, new_control, current_control)
        final_rows = jnp.dot(
            modulated(out_hidden, final_mod[0], final_mod[1]),
            final_weight,
            preferred_element_type=jnp.float32,
        )
        live_rows = (
            active & is_last_main & (share_start + jnp.arange(share_rows) < patch_length * TILE)
        )
        previous = lax.dynamic_slice_in_dim(denoised, row_start, share_rows, 0)
        denoised = lax.dynamic_update_slice_in_dim(
            denoised, jnp.where(live_rows[:, None], final_rows, previous), row_start, 0
        )
        inflow_hidden, inflow_control = from_behind((out_hidden, out_control), "section", HG)
        return (inflow_hidden, inflow_control, memory, denoised)

    empty_share = jnp.zeros((share_rows, D), jnp.bfloat16)
    initial = (
        empty_share,
        empty_share,
        memory_start,
        jnp.zeros((seq_rows + row_count, C_OUT), jnp.float32),
    )
    finished = lax.fori_loop(0, slot_count + PATCHES - 1, run_tick, initial)
    return lax.psum_scatter(finished[3][:seq_rows], "section", scatter_dimension=0, tiled=True)


def solution(mesh):
    return jax.shard_map(
        on_device,
        mesh=mesh,
        in_specs=(
            P(("grp", "section"), None),
            P(("grp", "section"), None),
            P(),
            P(),
            P(),
            P(),
            P(),
            P(),
            P(),
            P("section", None, None),
            P("section", None, None),
            P("section", "grp", None),
            P(),
            P(),
            P(),
        ),
        out_specs=P(("grp", "section"), None),
        check_vma=False,
    )
```

profile of v0, /device:TPU:0, one launch (start us, length us, event | category | flops | bytes accessed | tf_op | source)
XLA Modules:
  0.0 691.4 jit_solution(14145736935525604301)
XLA Ops:
  8.5 23.6 %all_gather.6 = bf16[768,64]{1,0:T(8,128)(2,1)S(1)} all-gather(bf16[48,64]{1,0:T(8,128)(2,1)S(1)} %copy-done.7), channel_id=1, replica_groups=mesh['grp'=2,'section'=16] {'section'}, dimensions={0}, use_global_device_ids=true | all-gather | bytes 104448 | tf_op jit(solution)/shard_map/all_gather | solution.py:134
  32.1 17.9 %all_gather.7 = bf16[768,64]{1,0:T(8,128)(2,1)S(1)} all-gather(bf16[48,64]{1,0:T(8,128)(2,1)S(1)} %copy-done.8), channel_id=1, replica_groups=mesh['grp'=2,'section'=16] {'section'}, dimensions={0}, use_global_device_ids=true | all-gather | bytes 104448 | tf_op jit(solution)/shard_map/all_gather | solution.py:135
  54.7 562.2 %while.25 = (s32[]{:T(128)}, bf16[32,3072]{1,0:T(8,128)(2,1)}, bf16[32,3072]{1,0:T(8,128)(2,1)S(1)}, bf16[1024,768]{0,1:T(8,128)(2,1)}, f32[1024,64]{1,0:T(8,128...) while((s32[]{:T(128)}, bf16[32,3072]{1,0:T(8,128)(2,1)}, ...), condition=%wide.region_12.13_spmd, body=%wide.region_1.12_spmd.sunk | while | flops 2714486016 | bytes 100601624 | solution.py:245
  62.3 9.7 %collective-permute-done.1 = bf16[64,3072]{1,0:T(8,128)(2,1)S(1)} collective-permute-done((bf16[64,3072]{1,0:T(8,128)(2,1)S(1)}, bf16[64,3072]{1,0:T(8,128)(2,1)S(1)}, u32[]{:S(2)}, u32[]{:S(2)}) %collective-permute-start.1) | collective-permute-done | bytes 393248 | tf_op jit(solution)/shard_map/while/body/eval_jaxpr/ppermute | solution.py:23
  73.0 18.3 %collective-permute-done.2 = bf16[128,3072]{1,0:T(8,128)(2,1)} collective-permute-done((bf16[128,3072]{1,0:T(8,128)(2,1)S(1)}, bf16[128,3072]{1,0:T(8,128)(2,1)}, u32[]{:S(2)}, u32[]{:S(2)}) %collective-permute-start.2) | collective-permute-done | bytes 786464 | tf_op jit(solution)/shard_map/while/body/eval_jaxpr/ppermute | solution.py:23
  93.4 25.1 %conditional.2 = (bf16[1024,768]{0,1:T(8,128)(2,1)}, bf16[128,3072]{1,0:T(8,128)(2,1)S(1)}, bf16[128,3072]{1,0:T(8,128)(2,1)S(1)}) conditional(s32[]{:T(128)} %convert_element_type.288, bf16[1024,768]{0,1:T(8,128)(2,1)} %get-tuple-element.1047, (s32[]{:T(128)}, pred[]{:T(512)}, bf16[256,3072]{1,0:T(8,128)(2,1)S(1)}, bf16[256,3072]{1,0:T(8,128)(2,1)S(1)}, ...), branch_computations={%region_2.2_spmd, %region_3.9_spmd} | conditional | flops 2658447616 | bytes 57946768 | solution.py:214
  95.3 6.2 fusion.7
  113.6 3.5 fusion.16
  118.9 17.8 %collective-permute-done.3 = bf16[128,3072]{1,0:T(8,128)(2,1)S(1)} collective-permute-done((bf16[128,3072]{1,0:T(8,128)(2,1)S(1)}, bf16[128,3072]{1,0:T(8,128)(2,1)S(1)}, u32[]{:S(2)}, u32[]{:S(2)}) %collective-permute-start.3) | collective-permute-done | bytes 786464 | tf_op jit(solution)/shard_map/while/body/eval_jaxpr/ppermute | solution.py:23
  138.9 7.0 %collective-permute-done.4 = bf16[64,3072]{1,0:T(8,128)(2,1)S(1)} collective-permute-done((bf16[64,3072]{1,0:T(8,128)(2,1)S(1)}, bf16[64,3072]{1,0:T(8,128)(2,1)S(1)}, u32[]{:S(2)}, u32[]{:S(2)}) %collective-permute-start.4) | collective-permute-done | bytes 393248 | tf_op jit(solution)/shard_map/while/body/eval_jaxpr/ppermute | solution.py:23
  154.4 3.7 collective-permute-done.7
  165.8 9.5 %collective-permute-done.1 = bf16[64,3072]{1,0:T(8,128)(2,1)S(1)} collective-permute-done((bf16[64,3072]{1,0:T(8,128)(2,1)S(1)}, bf16[64,3072]{1,0:T(8,128)(2,1)S(1)}, u32[]{:S(2)}, u32[]{:S(2)}) %collective-permute-start.1) | collective-permute-done | bytes 393248 | tf_op jit(solution)/shard_map/while/body/eval_jaxpr/ppermute | solution.py:23
  175.4 9.4 %collective-permute-start.2 = (bf16[128,3072]{1,0:T(8,128)(2,1)S(1)}, bf16[128,3072]{1,0:T(8,128)(2,1)}, u32[]{:S(2)}, u32[]{:S(2)}) collective-permute-start(bf16[128,3072]{1,0:T(8,128)(2,1)S(1)} %maximum_select_fusion.6), channel_id=1, source_target_pairs={{0,4},{1,5},{2,6},{3,7},{4,0},{5,1},{6,2},{7,3},{8,12},{9,13},{10,... | collective-permute-start | bytes 2359304 | tf_op jit(solution)/shard_map/while/body/eval_jaxpr/ppermute | solution.py:23
  185.5 16.5 %collective-permute-done.2 = bf16[128,3072]{1,0:T(8,128)(2,1)} collective-permute-done((bf16[128,3072]{1,0:T(8,128)(2,1)S(1)}, bf16[128,3072]{1,0:T(8,128)(2,1)}, u32[]{:S(2)}, u32[]{:S(2)}) %collective-permute-start.2) | collective-permute-done | bytes 786464 | tf_op jit(solution)/shard_map/while/body/eval_jaxpr/ppermute | solution.py:23
  204.0 25.1 %conditional.2 = (bf16[1024,768]{0,1:T(8,128)(2,1)}, bf16[128,3072]{1,0:T(8,128)(2,1)S(1)}, bf16[128,3072]{1,0:T(8,128)(2,1)S(1)}) conditional(s32[]{:T(128)} %convert_element_type.288, bf16[1024,768]{0,1:T(8,128)(2,1)} %get-tuple-element.1047, (s32[]{:T(128)}, pred[]{:T(512)}, bf16[256,3072]{1,0:T(8,128)(2,1)S(1)}, bf16[256,3072]{1,0:T(8,128)(2,1)S(1)}, ...), branch_computations={%region_2.2_spmd, %region_3.9_spmd} | conditional | flops 2658447616 | bytes 57946768 | solution.py:214
  205.9 6.2 fusion.7
  224.3 3.5 fusion.16
  231.0 16.4 %collective-permute-done.3 = bf16[128,3072]{1,0:T(8,128)(2,1)S(1)} collective-permute-done((bf16[128,3072]{1,0:T(8,128)(2,1)S(1)}, bf16[128,3072]{1,0:T(8,128)(2,1)S(1)}, u32[]{:S(2)}, u32[]{:S(2)}) %collective-permute-start.3) | collective-permute-done | bytes 786464 | tf_op jit(solution)/shard_map/while/body/eval_jaxpr/ppermute | solution.py:23
  249.6 7.1 %collective-permute-done.4 = bf16[64,3072]{1,0:T(8,128)(2,1)S(1)} collective-permute-done((bf16[64,3072]{1,0:T(8,128)(2,1)S(1)}, bf16[64,3072]{1,0:T(8,128)(2,1)S(1)}, u32[]{:S(2)}, u32[]{:S(2)}) %collective-permute-start.4) | collective-permute-done | bytes 393248 | tf_op jit(solution)/shard_map/while/body/eval_jaxpr/ppermute | solution.py:23
  258.7 6.0 collective-permute-start.6
  269.3 3.4 collective-permute-done.7
  280.3 9.5 %collective-permute-done.1 = bf16[64,3072]{1,0:T(8,128)(2,1)S(1)} collective-permute-done((bf16[64,3072]{1,0:T(8,128)(2,1)S(1)}, bf16[64,3072]{1,0:T(8,128)(2,1)S(1)}, u32[]{:S(2)}, u32[]{:S(2)}) %collective-permute-start.1) | collective-permute-done | bytes 393248 | tf_op jit(solution)/shard_map/while/body/eval_jaxpr/ppermute | solution.py:23
  290.0 9.6 %collective-permute-start.2 = (bf16[128,3072]{1,0:T(8,128)(2,1)S(1)}, bf16[128,3072]{1,0:T(8,128)(2,1)}, u32[]{:S(2)}, u32[]{:S(2)}) collective-permute-start(bf16[128,3072]{1,0:T(8,128)(2,1)S(1)} %maximum_select_fusion.6), channel_id=1, source_target_pairs={{0,4},{1,5},{2,6},{3,7},{4,0},{5,1},{6,2},{7,3},{8,12},{9,13},{10,... | collective-permute-start | bytes 2359304 | tf_op jit(solution)/shard_map/while/body/eval_jaxpr/ppermute | solution.py:23
  300.2 16.5 %collective-permute-done.2 = bf16[128,3072]{1,0:T(8,128)(2,1)} collective-permute-done((bf16[128,3072]{1,0:T(8,128)(2,1)S(1)}, bf16[128,3072]{1,0:T(8,128)(2,1)}, u32[]{:S(2)}, u32[]{:S(2)}) %collective-permute-start.2) | collective-permute-done | bytes 786464 | tf_op jit(solution)/shard_map/while/body/eval_jaxpr/ppermute | solution.py:23
  318.7 25.1 %conditional.2 = (bf16[1024,768]{0,1:T(8,128)(2,1)}, bf16[128,3072]{1,0:T(8,128)(2,1)S(1)}, bf16[128,3072]{1,0:T(8,128)(2,1)S(1)}) conditional(s32[]{:T(128)} %convert_element_type.288, bf16[1024,768]{0,1:T(8,128)(2,1)} %get-tuple-element.1047, (s32[]{:T(128)}, pred[]{:T(512)}, bf16[256,3072]{1,0:T(8,128)(2,1)S(1)}, bf16[256,3072]{1,0:T(8,128)(2,1)S(1)}, ...), branch_computations={%region_2.2_spmd, %region_3.9_spmd} | conditional | flops 2658447616 | bytes 57946768 | solution.py:214
  320.6 6.2 fusion.7
  339.0 3.5 fusion.16
  345.7 16.4 %collective-permute-done.3 = bf16[128,3072]{1,0:T(8,128)(2,1)S(1)} collective-permute-done((bf16[128,3072]{1,0:T(8,128)(2,1)S(1)}, bf16[128,3072]{1,0:T(8,128)(2,1)S(1)}, u32[]{:S(2)}, u32[]{:S(2)}) %collective-permute-start.3) | collective-permute-done | bytes 786464 | tf_op jit(solution)/shard_map/while/body/eval_jaxpr/ppermute | solution.py:23
  364.3 7.1 %collective-permute-done.4 = bf16[64,3072]{1,0:T(8,128)(2,1)S(1)} collective-permute-done((bf16[64,3072]{1,0:T(8,128)(2,1)S(1)}, bf16[64,3072]{1,0:T(8,128)(2,1)S(1)}, u32[]{:S(2)}, u32[]{:S(2)}) %collective-permute-start.4) | collective-permute-done | bytes 393248 | tf_op jit(solution)/shard_map/while/body/eval_jaxpr/ppermute | solution.py:23
  373.4 6.0 collective-permute-start.6
  384.0 3.4 collective-permute-done.7
  395.1 9.5 %collective-permute-done.1 = bf16[64,3072]{1,0:T(8,128)(2,1)S(1)} collective-permute-done((bf16[64,3072]{1,0:T(8,128)(2,1)S(1)}, bf16[64,3072]{1,0:T(8,128)(2,1)S(1)}, u32[]{:S(2)}, u32[]{:S(2)}) %collective-permute-start.1) | collective-permute-done | bytes 393248 | tf_op jit(solution)/shard_map/while/body/eval_jaxpr/ppermute | solution.py:23
  404.7 9.6 %collective-permute-start.2 = (bf16[128,3072]{1,0:T(8,128)(2,1)S(1)}, bf16[128,3072]{1,0:T(8,128)(2,1)}, u32[]{:S(2)}, u32[]{:S(2)}) collective-permute-start(bf16[128,3072]{1,0:T(8,128)(2,1)S(1)} %maximum_select_fusion.6), channel_id=1, source_target_pairs={{0,4},{1,5},{2,6},{3,7},{4,0},{5,1},{6,2},{7,3},{8,12},{9,13},{10,... | collective-permute-start | bytes 2359304 | tf_op jit(solution)/shard_map/while/body/eval_jaxpr/ppermute | solution.py:23
  415.0 16.5 %collective-permute-done.2 = bf16[128,3072]{1,0:T(8,128)(2,1)} collective-permute-done((bf16[128,3072]{1,0:T(8,128)(2,1)S(1)}, bf16[128,3072]{1,0:T(8,128)(2,1)}, u32[]{:S(2)}, u32[]{:S(2)}) %collective-permute-start.2) | collective-permute-done | bytes 786464 | tf_op jit(solution)/shard_map/while/body/eval_jaxpr/ppermute | solution.py:23
  433.5 25.1 %conditional.2 = (bf16[1024,768]{0,1:T(8,128)(2,1)}, bf16[128,3072]{1,0:T(8,128)(2,1)S(1)}, bf16[128,3072]{1,0:T(8,128)(2,1)S(1)}) conditional(s32[]{:T(128)} %convert_element_type.288, bf16[1024,768]{0,1:T(8,128)(2,1)} %get-tuple-element.1047, (s32[]{:T(128)}, pred[]{:T(512)}, bf16[256,3072]{1,0:T(8,128)(2,1)S(1)}, bf16[256,3072]{1,0:T(8,128)(2,1)S(1)}, ...), branch_computations={%region_2.2_spmd, %region_3.9_spmd} | conditional | flops 2658447616 | bytes 57946768 | solution.py:214
  435.4 6.2 fusion.7
  453.8 3.5 fusion.16
  460.5 16.4 %collective-permute-done.3 = bf16[128,3072]{1,0:T(8,128)(2,1)S(1)} collective-permute-done((bf16[128,3072]{1,0:T(8,128)(2,1)S(1)}, bf16[128,3072]{1,0:T(8,128)(2,1)S(1)}, u32[]{:S(2)}, u32[]{:S(2)}) %collective-permute-start.3) | collective-permute-done | bytes 786464 | tf_op jit(solution)/shard_map/while/body/eval_jaxpr/ppermute | solution.py:23
  479.1 7.1 %collective-permute-done.4 = bf16[64,3072]{1,0:T(8,128)(2,1)S(1)} collective-permute-done((bf16[64,3072]{1,0:T(8,128)(2,1)S(1)}, bf16[64,3072]{1,0:T(8,128)(2,1)S(1)}, u32[]{:S(2)}, u32[]{:S(2)}) %collective-permute-start.4) | collective-permute-done | bytes 393248 | tf_op jit(solution)/shard_map/while/body/eval_jaxpr/ppermute | solution.py:23
  488.1 6.0 collective-permute-start.6
  498.7 3.4 collective-permute-done.7
  509.8 9.5 %collective-permute-done.1 = bf16[64,3072]{1,0:T(8,128)(2,1)S(1)} collective-permute-done((bf16[64,3072]{1,0:T(8,128)(2,1)S(1)}, bf16[64,3072]{1,0:T(8,128)(2,1)S(1)}, u32[]{:S(2)}, u32[]{:S(2)}) %collective-permute-start.1) | collective-permute-done | bytes 393248 | tf_op jit(solution)/shard_map/while/body/eval_jaxpr/ppermute | solution.py:23
  519.4 9.6 %collective-permute-start.2 = (bf16[128,3072]{1,0:T(8,128)(2,1)S(1)}, bf16[128,3072]{1,0:T(8,128)(2,1)}, u32[]{:S(2)}, u32[]{:S(2)}) collective-permute-start(bf16[128,3072]{1,0:T(8,128)(2,1)S(1)} %maximum_select_fusion.6), channel_id=1, source_target_pairs={{0,4},{1,5},{2,6},{3,7},{4,0},{5,1},{6,2},{7,3},{8,12},{9,13},{10,... | collective-permute-start | bytes 2359304 | tf_op jit(solution)/shard_map/while/body/eval_jaxpr/ppermute | solution.py:23
  529.7 16.5 %collective-permute-done.2 = bf16[128,3072]{1,0:T(8,128)(2,1)} collective-permute-done((bf16[128,3072]{1,0:T(8,128)(2,1)S(1)}, bf16[128,3072]{1,0:T(8,128)(2,1)}, u32[]{:S(2)}, u32[]{:S(2)}) %collective-permute-start.2) | collective-permute-done | bytes 786464 | tf_op jit(solution)/shard_map/while/body/eval_jaxpr/ppermute | solution.py:23
  550.3 16.4 %collective-permute-done.3 = bf16[128,3072]{1,0:T(8,128)(2,1)S(1)} collective-permute-done((bf16[128,3072]{1,0:T(8,128)(2,1)S(1)}, bf16[128,3072]{1,0:T(8,128)(2,1)S(1)}, u32[]{:S(2)}, u32[]{:S(2)}) %collective-permute-start.3) | collective-permute-done | bytes 786464 | tf_op jit(solution)/shard_map/while/body/eval_jaxpr/ppermute | solution.py:23
  568.8 7.1 %collective-permute-done.4 = bf16[64,3072]{1,0:T(8,128)(2,1)S(1)} collective-permute-done((bf16[64,3072]{1,0:T(8,128)(2,1)S(1)}, bf16[64,3072]{1,0:T(8,128)(2,1)S(1)}, u32[]{:S(2)}, u32[]{:S(2)}) %collective-permute-start.4) | collective-permute-done | bytes 393248 | tf_op jit(solution)/shard_map/while/body/eval_jaxpr/ppermute | solution.py:23
  577.9 31.0 %collective-permute-start.6 = (bf16[32,3072]{1,0:T(8,128)(2,1)S(1)}, bf16[32,3072]{1,0:T(8,128)(2,1)}, u32[]{:S(2)}, u32[]{:S(2)}) collective-permute-start(bf16[32,3072]{1,0:T(8,128)(2,1)S(1)} %get-tuple-element.999), channel_id=1, source_target_pairs={{0,8},{1,9},{2,10},{3,11},{4,12},{5,13},{6,14},{7,15},{16,24},{17,... | collective-permute-start | bytes 589832 | tf_op jit(solution)/shard_map/while/body/eval_jaxpr/ppermute | solution.py:29
  618.7 65.8 %reduce-scatter.2.cloned.1.call-done = f32[48,64]{1,0:T(8,128)} async-done(((f32[768,64]{1,0:T(8,128)}), f32[48,64]{1,0:T(8,128)}) %reduce-scatter.2.cloned.1.call-update) | async-done | bytes 12304 | tf_op jit(solution)/shard_map/reduce_scatter | solution.py:246
  (378 shorter events, 167.0 us)
Async XLA Ops:
  6.5 43.5 %copy-start = (f32[2,3,3072]{2,0,1:T(2,128)S(1)}, f32[2,3,3072]{2,0,1:T(2,128)}, u32[]{:S(2)}) copy-start(f32[2,3,3072]{2,0,1:T(2,128)} %param.26) | copy-start | bytes 221188
  6.5 25.5 %copy-start.8 = (bf16[48,64]{1,0:T(8,128)(2,1)S(1)}, bf16[48,64]{1,0:T(8,128)(2,1)}, u32[]{:S(2)}) copy-start(bf16[48,64]{1,0:T(8,128)(2,1)} %param.20) | copy-start | bytes 18436
  6.5 43.6 %copy-start.10 = (f32[2,2,128]{2,1,0:T(2,128)S(1)}, f32[2,2,128]{2,1,0:T(2,128)}, u32[]{:S(2)}) copy-start(f32[2,2,128]{2,1,0:T(2,128)} %param.27) | copy-start | bytes 6148
  6.5 43.6 %copy-start.9 = (s32[2,6,3]{1,0,2:T(2,128)S(1)}, s32[2,6,3]{1,0,2:T(2,128)}, u32[]{:S(2)}) copy-start(s32[2,6,3]{1,0,2:T(2,128)} %param.22) | copy-start | bytes 436
  6.6 43.7 %copy-start.12 = (s32[2,6]{1,0:T(2,128)S(1)}, s32[2,6]{1,0:T(2,128)}, u32[]{:S(2)}) copy-start(s32[2,6]{1,0:T(2,128)} %param.23) | copy-start | bytes 148
  6.6 677.9 %reduce-scatter.2.cloned.1.call-start = ((), (), s32[]{:S(2)}) async-start(), calls=%async_computation.1 | async-start | bytes 417792 | tf_op jit(solution)/shard_map/reduce_scatter | solution.py:246
  59.0 1.4 collective-permute-start
  60.6 11.4 %collective-permute-start.1 = (bf16[64,3072]{1,0:T(8,128)(2,1)S(1)}, bf16[64,3072]{1,0:T(8,128)(2,1)S(1)}, u32[]{:S(2)}, u32[]{:S(2)}) collective-permute-start(bf16[64,3072]{1,0:T(8,128)(2,1)S(1)} %maximum_select_fusion.5), channel_id=1, source_target_pairs={{0,2},{1,3},{2,0},{3,1},{4,6},{5,7},{6,4},{7,5},{8,10},{9,11},{10,... | collective-permute-start | bytes 1179656 | tf_op jit(solution)/shard_map/while/body/eval_jaxpr/ppermute | solution.py:23
  72.2 19.2 %collective-permute-start.2 = (bf16[128,3072]{1,0:T(8,128)(2,1)S(1)}, bf16[128,3072]{1,0:T(8,128)(2,1)}, u32[]{:S(2)}, u32[]{:S(2)}) collective-permute-start(bf16[128,3072]{1,0:T(8,128)(2,1)S(1)} %maximum_select_fusion.6), channel_id=1, source_target_pairs={{0,4},{1,5},{2,6},{3,7},{4,0},{5,1},{6,2},{7,3},{8,12},{9,13},{10,... | collective-permute-start | bytes 2359304 | tf_op jit(solution)/shard_map/while/body/eval_jaxpr/ppermute | solution.py:23
  118.6 18.1 %collective-permute-start.3 = (bf16[128,3072]{1,0:T(8,128)(2,1)S(1)}, bf16[128,3072]{1,0:T(8,128)(2,1)S(1)}, u32[]{:S(2)}, u32[]{:S(2)}) collective-permute-start(bf16[128,3072]{1,0:T(8,128)(2,1)S(1)} %broadcast_select_fusion.7), channel_id=1, source_target_pairs={{0,4},{1,5},{2,6},{3,7},{4,0},{5,1},{6,2},{7,3},{8,12},{9,13},{10,... | collective-permute-start | bytes 2359304 | tf_op jit(solution)/shard_map/while/body/eval_jaxpr/ppermute | solution.py:23
  137.1 8.8 %collective-permute-start.4 = (bf16[64,3072]{1,0:T(8,128)(2,1)S(1)}, bf16[64,3072]{1,0:T(8,128)(2,1)S(1)}, u32[]{:S(2)}, u32[]{:S(2)}) collective-permute-start(bf16[64,3072]{1,0:T(8,128)(2,1)S(1)} %select_convert_fusion.4), channel_id=1, source_target_pairs={{0,2},{1,3},{2,0},{3,1},{4,6},{5,7},{6,4},{7,5},{8,10},{9,11},{10,... | collective-permute-start | bytes 1179656 | tf_op jit(solution)/shard_map/while/body/eval_jaxpr/ppermute | solution.py:23
  146.1 1.5 collective-permute-start.5
  147.9 6.5 collective-permute-start.6
  150.0 8.2 %collective-permute-start.7 = (bf16[32,3072]{1,0:T(8,128)(2,1)S(1)}, bf16[32,3072]{1,0:T(8,128)(2,1)S(1)}, u32[]{:S(2)}, u32[]{:S(2)}) collective-permute-start(bf16[32,3072]{1,0:T(8,128)(2,1)S(1)} %convert_select_fusion.4), channel_id=1, source_target_pairs={{0,8},{1,9},{2,10},{3,11},{4,12},{5,13},{6,14},{7,15},{16,24},{17,... | collective-permute-start | bytes 589832 | tf_op jit(solution)/shard_map/while/body/eval_jaxpr/ppermute | solution.py:29
  162.5 1.4 collective-permute-start
  164.1 11.2 %collective-permute-start.1 = (bf16[64,3072]{1,0:T(8,128)(2,1)S(1)}, bf16[64,3072]{1,0:T(8,128)(2,1)S(1)}, u32[]{:S(2)}, u32[]{:S(2)}) collective-permute-start(bf16[64,3072]{1,0:T(8,128)(2,1)S(1)} %maximum_select_fusion.5), channel_id=1, source_target_pairs={{0,2},{1,3},{2,0},{3,1},{4,6},{5,7},{6,4},{7,5},{8,10},{9,11},{10,... | collective-permute-start | bytes 1179656 | tf_op jit(solution)/shard_map/while/body/eval_jaxpr/ppermute | solution.py:23
  175.4 26.5 %collective-permute-start.2 = (bf16[128,3072]{1,0:T(8,128)(2,1)S(1)}, bf16[128,3072]{1,0:T(8,128)(2,1)}, u32[]{:S(2)}, u32[]{:S(2)}) collective-permute-start(bf16[128,3072]{1,0:T(8,128)(2,1)S(1)} %maximum_select_fusion.6), channel_id=1, source_target_pairs={{0,4},{1,5},{2,6},{3,7},{4,0},{5,1},{6,2},{7,3},{8,12},{9,13},{10,... | collective-permute-start | bytes 2359304 | tf_op jit(solution)/shard_map/while/body/eval_jaxpr/ppermute | solution.py:23
  229.2 18.2 %collective-permute-start.3 = (bf16[128,3072]{1,0:T(8,128)(2,1)S(1)}, bf16[128,3072]{1,0:T(8,128)(2,1)S(1)}, u32[]{:S(2)}, u32[]{:S(2)}) collective-permute-start(bf16[128,3072]{1,0:T(8,128)(2,1)S(1)} %broadcast_select_fusion.7), channel_id=1, source_target_pairs={{0,4},{1,5},{2,6},{3,7},{4,0},{5,1},{6,2},{7,3},{8,12},{9,13},{10,... | collective-permute-start | bytes 2359304 | tf_op jit(solution)/shard_map/while/body/eval_jaxpr/ppermute | solution.py:23
  247.8 8.8 %collective-permute-start.4 = (bf16[64,3072]{1,0:T(8,128)(2,1)S(1)}, bf16[64,3072]{1,0:T(8,128)(2,1)S(1)}, u32[]{:S(2)}, u32[]{:S(2)}) collective-permute-start(bf16[64,3072]{1,0:T(8,128)(2,1)S(1)} %select_convert_fusion.4), channel_id=1, source_target_pairs={{0,2},{1,3},{2,0},{3,1},{4,6},{5,7},{6,4},{7,5},{8,10},{9,11},{10,... | collective-permute-start | bytes 1179656 | tf_op jit(solution)/shard_map/while/body/eval_jaxpr/ppermute | solution.py:23
  256.9 1.5 collective-permute-start.5
  258.7 10.6 %collective-permute-start.6 = (bf16[32,3072]{1,0:T(8,128)(2,1)S(1)}, bf16[32,3072]{1,0:T(8,128)(2,1)}, u32[]{:S(2)}, u32[]{:S(2)}) collective-permute-start(bf16[32,3072]{1,0:T(8,128)(2,1)S(1)} %get-tuple-element.999), channel_id=1, source_target_pairs={{0,8},{1,9},{2,10},{3,11},{4,12},{5,13},{6,14},{7,15},{16,24},{17,... | collective-permute-start | bytes 589832 | tf_op jit(solution)/shard_map/while/body/eval_jaxpr/ppermute | solution.py:29
  264.8 7.9 %collective-permute-start.7 = (bf16[32,3072]{1,0:T(8,128)(2,1)S(1)}, bf16[32,3072]{1,0:T(8,128)(2,1)S(1)}, u32[]{:S(2)}, u32[]{:S(2)}) collective-permute-start(bf16[32,3072]{1,0:T(8,128)(2,1)S(1)} %convert_select_fusion.4), channel_id=1, source_target_pairs={{0,8},{1,9},{2,10},{3,11},{4,12},{5,13},{6,14},{7,15},{16,24},{17,... | collective-permute-start | bytes 589832 | tf_op jit(solution)/shard_map/while/body/eval_jaxpr/ppermute | solution.py:29
  277.1 1.4 collective-permute-start
  278.6 11.2 %collective-permute-start.1 = (bf16[64,3072]{1,0:T(8,128)(2,1)S(1)}, bf16[64,3072]{1,0:T(8,128)(2,1)S(1)}, u32[]{:S(2)}, u32[]{:S(2)}) collective-permute-start(bf16[64,3072]{1,0:T(8,128)(2,1)S(1)} %maximum_select_fusion.5), channel_id=1, source_target_pairs={{0,2},{1,3},{2,0},{3,1},{4,6},{5,7},{6,4},{7,5},{8,10},{9,11},{10,... | collective-permute-start | bytes 1179656 | tf_op jit(solution)/shard_map/while/body/eval_jaxpr/ppermute | solution.py:23
  290.0 26.7 %collective-permute-start.2 = (bf16[128,3072]{1,0:T(8,128)(2,1)S(1)}, bf16[128,3072]{1,0:T(8,128)(2,1)}, u32[]{:S(2)}, u32[]{:S(2)}) collective-permute-start(bf16[128,3072]{1,0:T(8,128)(2,1)S(1)} %maximum_select_fusion.6), channel_id=1, source_target_pairs={{0,4},{1,5},{2,6},{3,7},{4,0},{5,1},{6,2},{7,3},{8,12},{9,13},{10,... | collective-permute-start | bytes 2359304 | tf_op jit(solution)/shard_map/while/body/eval_jaxpr/ppermute | solution.py:23
  343.9 18.2 %collective-permute-start.3 = (bf16[128,3072]{1,0:T(8,128)(2,1)S(1)}, bf16[128,3072]{1,0:T(8,128)(2,1)S(1)}, u32[]{:S(2)}, u32[]{:S(2)}) collective-permute-start(bf16[128,3072]{1,0:T(8,128)(2,1)S(1)} %broadcast_select_fusion.7), channel_id=1, source_target_pairs={{0,4},{1,5},{2,6},{3,7},{4,0},{5,1},{6,2},{7,3},{8,12},{9,13},{10,... | collective-permute-start | bytes 2359304 | tf_op jit(solution)/shard_map/while/body/eval_jaxpr/ppermute | solution.py:23
  362.5 8.8 %collective-permute-start.4 = (bf16[64,3072]{1,0:T(8,128)(2,1)S(1)}, bf16[64,3072]{1,0:T(8,128)(2,1)S(1)}, u32[]{:S(2)}, u32[]{:S(2)}) collective-permute-start(bf16[64,3072]{1,0:T(8,128)(2,1)S(1)} %select_convert_fusion.4), channel_id=1, source_target_pairs={{0,2},{1,3},{2,0},{3,1},{4,6},{5,7},{6,4},{7,5},{8,10},{9,11},{10,... | collective-permute-start | bytes 1179656 | tf_op jit(solution)/shard_map/while/body/eval_jaxpr/ppermute | solution.py:23
  371.6 1.5 collective-permute-start.5
  373.4 10.6 %collective-permute-start.6 = (bf16[32,3072]{1,0:T(8,128)(2,1)S(1)}, bf16[32,3072]{1,0:T(8,128)(2,1)}, u32[]{:S(2)}, u32[]{:S(2)}) collective-permute-start(bf16[32,3072]{1,0:T(8,128)(2,1)S(1)} %get-tuple-element.999), channel_id=1, source_target_pairs={{0,8},{1,9},{2,10},{3,11},{4,12},{5,13},{6,14},{7,15},{16,24},{17,... | collective-permute-start | bytes 589832 | tf_op jit(solution)/shard_map/while/body/eval_jaxpr/ppermute | solution.py:29
  379.5 7.9 %collective-permute-start.7 = (bf16[32,3072]{1,0:T(8,128)(2,1)S(1)}, bf16[32,3072]{1,0:T(8,128)(2,1)S(1)}, u32[]{:S(2)}, u32[]{:S(2)}) collective-permute-start(bf16[32,3072]{1,0:T(8,128)(2,1)S(1)} %convert_select_fusion.4), channel_id=1, source_target_pairs={{0,8},{1,9},{2,10},{3,11},{4,12},{5,13},{6,14},{7,15},{16,24},{17,... | collective-permute-start | bytes 589832 | tf_op jit(solution)/shard_map/while/body/eval_jaxpr/ppermute | solution.py:29
  391.8 1.4 collective-permute-start
  393.3 11.2 %collective-permute-start.1 = (bf16[64,3072]{1,0:T(8,128)(2,1)S(1)}, bf16[64,3072]{1,0:T(8,128)(2,1)S(1)}, u32[]{:S(2)}, u32[]{:S(2)}) collective-permute-start(bf16[64,3072]{1,0:T(8,128)(2,1)S(1)} %maximum_select_fusion.5), channel_id=1, source_target_pairs={{0,2},{1,3},{2,0},{3,1},{4,6},{5,7},{6,4},{7,5},{8,10},{9,11},{10,... | collective-permute-start | bytes 1179656 | tf_op jit(solution)/shard_map/while/body/eval_jaxpr/ppermute | solution.py:23
  404.7 26.7 %collective-permute-start.2 = (bf16[128,3072]{1,0:T(8,128)(2,1)S(1)}, bf16[128,3072]{1,0:T(8,128)(2,1)}, u32[]{:S(2)}, u32[]{:S(2)}) collective-permute-start(bf16[128,3072]{1,0:T(8,128)(2,1)S(1)} %maximum_select_fusion.6), channel_id=1, source_target_pairs={{0,4},{1,5},{2,6},{3,7},{4,0},{5,1},{6,2},{7,3},{8,12},{9,13},{10,... | collective-permute-start | bytes 2359304 | tf_op jit(solution)/shard_map/while/body/eval_jaxpr/ppermute | solution.py:23
  458.7 18.2 %collective-permute-start.3 = (bf16[128,3072]{1,0:T(8,128)(2,1)S(1)}, bf16[128,3072]{1,0:T(8,128)(2,1)S(1)}, u32[]{:S(2)}, u32[]{:S(2)}) collective-permute-start(bf16[128,3072]{1,0:T(8,128)(2,1)S(1)} %broadcast_select_fusion.7), channel_id=1, source_target_pairs={{0,4},{1,5},{2,6},{3,7},{4,0},{5,1},{6,2},{7,3},{8,12},{9,13},{10,... | collective-permute-start | bytes 2359304 | tf_op jit(solution)/shard_map/while/body/eval_jaxpr/ppermute | solution.py:23
  477.3 10.6 %copy-start.3 = (bf16[32,3072]{1,0:T(8,128)(2,1)S(1)}, bf16[32,3072]{1,0:T(8,128)(2,1)}, u32[]{:S(2)}) copy-start(bf16[32,3072]{1,0:T(8,128)(2,1)} %get-tuple-element.993) | copy-start | bytes 589828 | tf_op jit(solution)/shard_map/while
  477.3 8.9 %collective-permute-start.4 = (bf16[64,3072]{1,0:T(8,128)(2,1)S(1)}, bf16[64,3072]{1,0:T(8,128)(2,1)S(1)}, u32[]{:S(2)}, u32[]{:S(2)}) collective-permute-start(bf16[64,3072]{1,0:T(8,128)(2,1)S(1)} %select_convert_fusion.4), channel_id=1, source_target_pairs={{0,2},{1,3},{2,0},{3,1},{4,6},{5,7},{6,4},{7,5},{8,10},{9,11},{10,... | collective-permute-start | bytes 1179656 | tf_op jit(solution)/shard_map/while/body/eval_jaxpr/ppermute | solution.py:23
  486.4 1.5 collective-permute-start.5
  488.1 10.6 %collective-permute-start.6 = (bf16[32,3072]{1,0:T(8,128)(2,1)S(1)}, bf16[32,3072]{1,0:T(8,128)(2,1)}, u32[]{:S(2)}, u32[]{:S(2)}) collective-permute-start(bf16[32,3072]{1,0:T(8,128)(2,1)S(1)} %get-tuple-element.999), channel_id=1, source_target_pairs={{0,8},{1,9},{2,10},{3,11},{4,12},{5,13},{6,14},{7,15},{16,24},{17,... | collective-permute-start | bytes 589832 | tf_op jit(solution)/shard_map/while/body/eval_jaxpr/ppermute | solution.py:29
  494.3 7.9 %collective-permute-start.7 = (bf16[32,3072]{1,0:T(8,128)(2,1)S(1)}, bf16[32,3072]{1,0:T(8,128)(2,1)S(1)}, u32[]{:S(2)}, u32[]{:S(2)}) collective-permute-start(bf16[32,3072]{1,0:T(8,128)(2,1)S(1)} %convert_select_fusion.4), channel_id=1, source_target_pairs={{0,8},{1,9},{2,10},{3,11},{4,12},{5,13},{6,14},{7,15},{16,24},{17,... | collective-permute-start | bytes 589832 | tf_op jit(solution)/shard_map/while/body/eval_jaxpr/ppermute | solution.py:29
  506.5 1.4 collective-permute-start
  508.0 11.2 %collective-permute-start.1 = (bf16[64,3072]{1,0:T(8,128)(2,1)S(1)}, bf16[64,3072]{1,0:T(8,128)(2,1)S(1)}, u32[]{:S(2)}, u32[]{:S(2)}) collective-permute-start(bf16[64,3072]{1,0:T(8,128)(2,1)S(1)} %maximum_select_fusion.5), channel_id=1, source_target_pairs={{0,2},{1,3},{2,0},{3,1},{4,6},{5,7},{6,4},{7,5},{8,10},{9,11},{10,... | collective-permute-start | bytes 1179656 | tf_op jit(solution)/shard_map/while/body/eval_jaxpr/ppermute | solution.py:23
  519.4 26.7 %collective-permute-start.2 = (bf16[128,3072]{1,0:T(8,128)(2,1)S(1)}, bf16[128,3072]{1,0:T(8,128)(2,1)}, u32[]{:S(2)}, u32[]{:S(2)}) collective-permute-start(bf16[128,3072]{1,0:T(8,128)(2,1)S(1)} %maximum_select_fusion.6), channel_id=1, source_target_pairs={{0,4},{1,5},{2,6},{3,7},{4,0},{5,1},{6,2},{7,3},{8,12},{9,13},{10,... | collective-permute-start | bytes 2359304 | tf_op jit(solution)/shard_map/while/body/eval_jaxpr/ppermute | solution.py:23
  548.5 18.2 %collective-permute-start.3 = (bf16[128,3072]{1,0:T(8,128)(2,1)S(1)}, bf16[128,3072]{1,0:T(8,128)(2,1)S(1)}, u32[]{:S(2)}, u32[]{:S(2)}) collective-permute-start(bf16[128,3072]{1,0:T(8,128)(2,1)S(1)} %broadcast_select_fusion.7), channel_id=1, source_target_pairs={{0,4},{1,5},{2,6},{3,7},{4,0},{5,1},{6,2},{7,3},{8,12},{9,13},{10,... | collective-permute-start | bytes 2359304 | tf_op jit(solution)/shard_map/while/body/eval_jaxpr/ppermute | solution.py:23
  567.1 8.8 %collective-permute-start.4 = (bf16[64,3072]{1,0:T(8,128)(2,1)S(1)}, bf16[64,3072]{1,0:T(8,128)(2,1)S(1)}, u32[]{:S(2)}, u32[]{:S(2)}) collective-permute-start(bf16[64,3072]{1,0:T(8,128)(2,1)S(1)} %select_convert_fusion.4), channel_id=1, source_target_pairs={{0,2},{1,3},{2,0},{3,1},{4,6},{5,7},{6,4},{7,5},{8,10},{9,11},{10,... | collective-permute-start | bytes 1179656 | tf_op jit(solution)/shard_map/while/body/eval_jaxpr/ppermute | solution.py:23
  576.1 1.5 collective-permute-start.5
  577.6 32.9 %copy-start.11 = (bf16[3072,64]{0,1:T(8,128)(2,1)S(1)}, bf16[3072,64]{0,1:T(8,128)(2,1)}, u32[]{:S(2)}) copy-start(bf16[3072,64]{0,1:T(8,128)(2,1)} %get-tuple-element.1105) | copy-start | bytes 1179652 | tf_op jit(solution)/shard_map/while
  577.9 35.6 %collective-permute-start.6 = (bf16[32,3072]{1,0:T(8,128)(2,1)S(1)}, bf16[32,3072]{1,0:T(8,128)(2,1)}, u32[]{:S(2)}, u32[]{:S(2)}) collective-permute-start(bf16[32,3072]{1,0:T(8,128)(2,1)S(1)} %get-tuple-element.999), channel_id=1, source_target_pairs={{0,8},{1,9},{2,10},{3,11},{4,12},{5,13},{6,14},{7,15},{16,24},{17,... | collective-permute-start | bytes 589832 | tf_op jit(solution)/shard_map/while/body/eval_jaxpr/ppermute | solution.py:29
  609.0 7.9 %collective-permute-start.7 = (bf16[32,3072]{1,0:T(8,128)(2,1)S(1)}, bf16[32,3072]{1,0:T(8,128)(2,1)S(1)}, u32[]{:S(2)}, u32[]{:S(2)}) collective-permute-start(bf16[32,3072]{1,0:T(8,128)(2,1)S(1)} %convert_select_fusion.4), channel_id=1, source_target_pairs={{0,8},{1,9},{2,10},{3,11},{4,12},{5,13},{6,14},{7,15},{16,24},{17,... | collective-permute-start | bytes 589832 | tf_op jit(solution)/shard_map/while/body/eval_jaxpr/ppermute | solution.py:29
  (25 other events, 140.4 us)
Sparse Core Ops, SparseCore 0:
  618.8 65.6 reduce-scatter.1
where the time goes:
time: 693 us; the launch traced here: 691 us
  waiting for transfers between devices  351 us (51%)
  starting transfers between devices  121 us (17%)
  matrix products  75.3 us (11%)
  blocking collectives  41.6 us (6%)
  local copies, waits for them, and re-layouts  38.4 us (6%)
  other arithmetic  37.4 us (5%)
  between operations  13.5 us (2%)
  loops' own time  13 us (2%)
    ppermute x30, waiting for transfers between devices, from_partner(): lax.ppermute(value, axis, [(i, i ^ 1 << distance) for i in range(lax.axis...  261 us
    reduce_scatter x1, waiting for transfers between devices, on_device(): lax.psum_scatter(finished[3][:seq_rows], 'section', scatter_dimension=0,...  65.8 us
    ppermute x30, starting transfers between devices, from_partner(): lax.ppermute(value, axis, [(i, i ^ 1 << distance) for i in range(lax.axis...  63.9 us
    ppermute x10, starting transfers between devices, from_behind(): lax.ppermute(value, axis, [(source, source + steps) for source in range(l...  57.5 us
    dot_general x4, matrix products, attend_group(): jnp.dot(modded, w_qkv, preferred_element_type=jnp.float32)  24.9 us
    ppermute x10, waiting for transfers between devices, from_behind(): lax.ppermute(value, axis, [(source, source + steps) for source in range(l...  23.7 us
    all_gather x1, blocking collectives, on_device(): lax.all_gather(latent, 'section', axis=0, tiled=True)  23.6 us
    all_gather x1, blocking collectives, on_device(): lax.all_gather(control_latent, 'section', axis=0, tiled=True)  17.9 us
  transfers between devices with their start and end apart: 41, of which 41 were waited for; matrix products, arithmetic and copies ran while one was open for 2% of the time, Pallas kernels for 0%

commit v1 on v0

v1 whole, which is shorter than its diff:
```python
import functools
import math

import jax
import jax.numpy as jnp
from jax import lax
from jax.experimental import pallas as pl
from jax.experimental.pallas import tpu as pltpu
from jax.sharding import PartitionSpec as P

HD = 128
HG = 8
TILE = 128
EPSILON = 1e-06
CHUNKS = 6
Y_FIRST = (True, True, False, True, True, False)
MESH = pl.DeviceIdType.MESH


def normed(values, shift_row, scale_row):
    centered = values - jnp.mean(values, axis=-1, keepdims=True)
    variance = jnp.mean(centered * centered, axis=-1, keepdims=True)
    return centered * lax.rsqrt(variance + EPSILON) * (1.0 + scale_row) + shift_row


def modulated(hidden, shift_row, scale_row):
    return normed(hidden.astype(jnp.float32), shift_row, scale_row).astype(jnp.bfloat16)


def rms_scaled(values, gain_row):
    return (
        values * lax.rsqrt(jnp.mean(values * values, axis=-1, keepdims=True) + EPSILON) * gain_row
    )


def attend_kernel(
    embeds,
    patch_tiles,
    tile_lists,
    tile_counts,
    modulation,
    qk_gain,
    w_qkv_hbm,
    stale_hbm,
    *rest,
):
    *sources, out, w_qkv, modded, queries, memory, w_sem, stale_sem = rest
    slot = lax.axis_index("section") // HG
    tiles = stale_hbm.shape[0]
    features = out.shape[1]
    heads = features // HD
    copies = []
    for part in range(3):
        columns = pl.ds(part * features, features)
        copies.append(
            pltpu.make_async_copy(
                w_qkv_hbm.at[:, columns], w_qkv.at[:, columns], w_sem.at[part]
            )
        )
        copies[-1].start()
    stale_copy = pltpu.make_async_copy(stale_hbm, memory.at[pl.ds(tiles, tiles)], stale_sem)
    stale_copy.start()

    for tile in range(tiles):
        rows = slice(tile * TILE, (tile + 1) * TILE)
        if embeds:
            latent, control_latent, embed_weight, control_embed = sources
            values = jnp.dot(
                latent[rows], embed_weight[...], preferred_element_type=jnp.float32
            ) + jnp.dot(
                control_latent[rows], control_embed[...], preferred_element_type=jnp.float32
            )
            values = values.astype(jnp.bfloat16)
        else:
            values = sources[0][rows]
        modded[rows] = modulated(values, modulation[slot, 0:1], modulation[slot, 1:2])

    for part in range(3):
        copies[part].wait()
        projected = jnp.dot(
            modded[...],
            w_qkv[:, part * features : (part + 1) * features],
            preferred_element_type=jnp.float32,
        )
        for head in range(heads):
            columns = slice(head * HD, (head + 1) * HD)
            values = projected[:, columns]
            if part < 2:
                values = rms_scaled(values, qk_gain[slot, part : part + 1])
            values = values.astype(jnp.bfloat16)
            if part == 0:
                queries[:, columns] = values
            else:
                offset = (part - 1) * features + head * HD
                memory[0:tiles, :, offset : offset + HD] = values.reshape(tiles, TILE, HD)
    stale_copy.wait()

    def patch_of(tile):
        end, patch = 0, 0
        for p in range(patch_tiles.shape[0]):
            end = end + patch_tiles[p]
            patch = patch + jnp.where(tile >= end, 1, 0)
        return patch

    for tile in range(tiles):
        rows = slice(tile * TILE, (tile + 1) * TILE)
        own_patch = patch_of(tile)
        listed = []
        for j in range(tile_lists.shape[2]):
            key_tile = tile_lists[slot, tile, j]
            listed.append(key_tile + jnp.where(patch_of(key_tile) <= own_patch, 0, tiles))
        used = tile_counts[slot, tile]
        for head in range(heads):
            columns = slice(head * HD, (head + 1) * HD)
            query = queries[rows, columns]
            scores = []
            for j, place in enumerate(listed):
                score = lax.dot_general(
                    query,
                    memory[place, :, columns],
                    (((1,), (1,)), ((), ())),
                    preferred_element_type=jnp.float32,
                ) / math.sqrt(HD)
                scores.append(jnp.where(j < used, score, -1e30))
            scores = jnp.concatenate(scores, axis=1)
            weights = jnp.exp(scores - jnp.max(scores, axis=-1, keepdims=True))
            probabilities = (weights / jnp.sum(weights, axis=-1, keepdims=True)).astype(
                jnp.bfloat16
            )
            value_columns = slice(features + head * HD, features + (head + 1) * HD)
            value_rows = jnp.concatenate([memory[place, :, value_columns] for place in listed])
            out[rows, columns] = jnp.dot(
                probabilities, value_rows, preferred_element_type=jnp.float32
            ).astype(jnp.bfloat16)


def attended_of(
    sources, patch_tiles, tile_lists, tile_counts, modulation, qk_gain, w_qkv, stale
):
    row_count, kv = stale.shape
    width, columns = w_qkv.shape
    tiles = row_count // TILE
    whole = pl.BlockSpec(memory_space=pltpu.VMEM)
    scalars = pl.BlockSpec(memory_space=pltpu.SMEM)
    far = pl.BlockSpec(memory_space=pl.ANY)
    return pl.pallas_call(
        functools.partial(attend_kernel, len(sources) == 4),
        out_shape=jax.ShapeDtypeStruct((row_count, kv // 2), jnp.bfloat16),
        in_specs=[scalars] * 3 + [whole] * 2 + [far] * 2 + [whole] * len(sources),
        out_specs=whole,
        scratch_shapes=[
            pltpu.VMEM((width, columns), jnp.bfloat16),
            pltpu.VMEM((row_count, width), jnp.bfloat16),
            pltpu.VMEM((row_count, kv // 2), jnp.bfloat16),
            pltpu.VMEM((2 * tiles, TILE, kv), jnp.bfloat16),
            pltpu.SemaphoreType.DMA((3,)),
            pltpu.SemaphoreType.DMA,
        ],
        compiler_params=pltpu.CompilerParams(vmem_limit_bytes=40 * 2**20),
        cost_estimate=pl.CostEstimate(
            flops=6 * 10**9, bytes_accessed=10**7, transcendentals=10**6
        ),
        name="attend",
    )(
        patch_tiles,
        tile_lists,
        tile_counts,
        modulation,
        qk_gain,
        w_qkv,
        stale.reshape(tiles, TILE, kv),
        *sources,
    )


def reduce_kernel(
    attended,
    w_out,
    modulation,
    control_gain,
    latent,
    control_latent,
    embed_weight,
    control_embed,
    tail,
    final_weight,
    out,
    contrib,
    total,
    gate,
    got0,
    got1,
    got2,
    got3,
    give1,
    give2,
    give3,
    send_sem,
    recv_sem,
):
    chunks = contrib.shape[0]
    share, width = contrib.shape[-2:]
    grp = lax.axis_index("grp")
    me = lax.axis_index("section")
    core, y_bit, z_bit, slot = me % 2, me // 2 % 2, me // 4 % 2, me // 8
    others = {
        "core": me + 1 - 2 * core,
        "y": me + 2 - 4 * y_bit,
        "z": me + 4 - 8 * z_bit,
        "slot": me + 8 - 16 * slot,
    }
    barrier = pltpu.get_barrier_semaphore()
    for other in others.values():
        pl.semaphore_signal(barrier, inc=1, device_id=(grp, other), device_id_type=MESH)
    gate[...] = modulation[slot, 2:3] * jnp.where(slot == 0, control_gain[0:1], 1.0)
    pl.semaphore_wait(barrier, 4)

    def exchange(stage, k, src, dst, other):
        return pltpu.make_async_remote_copy(
            src_ref=src,
            dst_ref=dst,
            send_sem=send_sem.at[stage, k],
            recv_sem=recv_sem.at[stage, k],
            device_id=(grp, other),
            device_id_type=MESH,
        )

    pending = {}

    def embedded(columns):
        plain = jnp.dot(
            latent[...], embed_weight[:, columns], preferred_element_type=jnp.float32
        )
        control = plain + jnp.dot(
            control_latent[...], control_embed[:, columns], preferred_element_type=jnp.float32
        )
        control = control.astype(jnp.bfloat16).astype(jnp.float32)
        return plain.astype(jnp.bfloat16).astype(jnp.float32) + control_gain[0:1, columns] * control

    def stage0(k):
        columns = slice(k * width, (k + 1) * width)
        part = jnp.dot(attended[...], w_out[:, columns], preferred_element_type=jnp.float32)
        part = (part * gate[:, columns]).astype(jnp.bfloat16)
        for block in range(16):
            s, zb, yb, c = block >> 3, block >> 2 & 1, block >> 1 & 1, block & 1
            first, second = (yb, zb) if Y_FIRST[k] else (zb, yb)
            contrib[k, c, first, second, s] = part[block * share : (block + 1) * share]
        pending[0, k] = exchange(0, k, contrib.at[k, 1 - core], got0.at[k], others["core"])
        pending[0, k].start()

    def later(stage, k):
        pending[stage - 1, k].wait()
        first, second = (y_bit, z_bit) if Y_FIRST[k] else (z_bit, y_bit)
        names = ("y", "z") if Y_FIRST[k] else ("z", "y")
        if stage == 1:
            for half, to in ((1 - first, give1.at[k]), (first, None)):
                summed = contrib[k, core, half].astype(jnp.float32) + got0[k, half].astype(
                    jnp.float32
                )
                if to is None:
                    contrib[k, core, half] = summed.astype(jnp.bfloat16)
                else:
                    to[...] = summed.astype(jnp.bfloat16)
                    pending[1, k] = exchange(1, k, to, got1.at[k], others[names[0]])
                    pending[1, k].start()
        elif stage == 2:
            for half, to in ((1 - second, give2.at[k]), (second, None)):
                summed = contrib[k, core, first, half].astype(jnp.float32) + got1[
                    k, half
                ].astype(jnp.float32)
                if to is None:
                    contrib[k, core, first, half] = summed.astype(jnp.bfloat16)
                else:
                    to[...] = summed.astype(jnp.bfloat16)
                    pending[2, k] = exchange(2, k, to, got2.at[k], others[names[1]])
                    pending[2, k].start()
        elif stage == 3:
            for half, to in ((1 - slot, give3.at[k]), (slot, None)):
                summed = contrib[k, core, first, second, half].astype(jnp.float32) + got2[
                    k, half
                ].astype(jnp.float32)
                if to is None:
                    columns = slice(k * width, (k + 1) * width)
                    total[:, columns] = summed + embedded(columns)
                else:
                    to[...] = summed.astype(jnp.bfloat16)
                    pending[3, k] = exchange(3, k, to, got3.at[k], others["slot"])
                    pending[3, k].start()
        else:
            columns = slice(k * width, (k + 1) * width)
            total[:, columns] = (
                total[:, columns] + got3[k].astype(jnp.float32)
            )

    for step in range(chunks + 4):
        for stage in range(4, 0, -1):
            if 0 <= step - stage < chunks:
                later(stage, step - stage)
        if step < chunks:
            stage0(step)

    hidden = total[...].astype(jnp.bfloat16).astype(jnp.float32)
    modded = normed(hidden, tail[0:1], tail[1:2]).astype(jnp.bfloat16)
    out[...] = jnp.dot(modded, final_weight[...], preferred_element_type=jnp.float32)


def reduced(
    attended,
    w_out,
    modulation,
    control_gain,
    latent,
    control_latent,
    embed_weight,
    control_embed,
    final_mod,
    final_weight,
):
    share, width = latent.shape[0], w_out.shape[1]
    cw = width // CHUNKS
    bf = jnp.bfloat16
    whole = pl.BlockSpec(memory_space=pltpu.VMEM)
    return pl.pallas_call(
        reduce_kernel,
        out_shape=jax.ShapeDtypeStruct((share, final_weight.shape[1]), jnp.float32),
        in_specs=[whole] * 10,
        out_specs=whole,
        scratch_shapes=[
            pltpu.VMEM((CHUNKS, 2, 2, 2, 2, share, cw), bf),
            pltpu.VMEM((share, width), jnp.float32),
            pltpu.VMEM((1, width), jnp.float32),
            pltpu.VMEM((CHUNKS, 2, 2, 2, share, cw), bf),
            pltpu.VMEM((CHUNKS, 2, 2, share, cw), bf),
            pltpu.VMEM((CHUNKS, 2, share, cw), bf),
            pltpu.VMEM((CHUNKS, share, cw), bf),
            pltpu.VMEM((CHUNKS, 2, 2, share, cw), bf),
            pltpu.VMEM((CHUNKS, 2, share, cw), bf),
            pltpu.VMEM((CHUNKS, share, cw), bf),
            pltpu.SemaphoreType.DMA((4, CHUNKS)),
            pltpu.SemaphoreType.DMA((4, CHUNKS)),
        ],
        compiler_params=pltpu.CompilerParams(
            collective_id=0, has_side_effects=True, vmem_limit_bytes=48 * 2**20
        ),
        cost_estimate=pl.CostEstimate(flops=2 * 10**9, bytes_accessed=10**7, transcendentals=0),
        name="reduce_rows",
    )(
        attended,
        w_out,
        modulation,
        control_gain,
        latent,
        control_latent,
        embed_weight,
        control_embed,
        final_mod,
        final_weight,
    )


def gathered(rows):
    me = lax.axis_index("section")
    count = lax.axis_size("section")
    step = 1
    while step < count:
        partner = lax.ppermute(rows, "section", [(i, i ^ step) for i in range(count)])
        upper = me // step % 2 == 1
        rows = jnp.concatenate(
            [jnp.where(upper, partner, rows), jnp.where(upper, rows, partner)]
        )
        step *= 2
    return rows


def embed(latent, control_latent, embed_weight, control_embed):
    embedded = jnp.dot(latent, embed_weight, preferred_element_type=jnp.float32)
    conditioned = embedded + jnp.dot(
        control_latent, control_embed, preferred_element_type=jnp.float32
    )
    return embedded.astype(jnp.bfloat16), conditioned.astype(jnp.bfloat16)


def on_device(
    latent,
    control_latent,
    patch_tiles,
    tile_lists,
    tile_counts,
    embed_weight,
    control_embed,
    modulation,
    qk_gain,
    qkv_weight,
    out_weight,
    stale_cache,
    control_gain,
    final_mod,
    final_weight,
):
    count = lax.axis_size("section")
    slot_count = count // HG
    me = lax.axis_index("section")
    slot = me // HG
    is_control = slot % 2 == 0
    def attended(*sources):
        return attended_of(
            sources,
            patch_tiles,
            tile_lists,
            tile_counts,
            modulation,
            qk_gain,
            qkv_weight[0],
            stale_cache[0],
        )

    if slot_count == 2:
        both = gathered(jnp.concatenate([latent, control_latent], axis=1))
        half = latent.shape[1]
        whole_latent, whole_control = both[:, :half], both[:, half:]
        used_control = jnp.where(is_control, whole_control, jnp.zeros_like(whole_control))
        return reduced(
            attended(whole_latent, used_control, embed_weight, control_embed),
            out_weight[0],
            modulation,
            control_gain,
            latent,
            control_latent,
            embed_weight,
            control_embed,
            final_mod,
            final_weight,
        )

    def level_of(level, own):
        own_hidden, own_control = own
        rows = jnp.where(
            is_control,
            lax.all_gather(own_control, "section", axis=0, tiled=True),
            lax.all_gather(own_hidden, "section", axis=0, tiled=True),
        )
        partial_value = jnp.dot(
            attended(rows), out_weight[0], preferred_element_type=jnp.float32
        ).astype(jnp.bfloat16)

        def summed(of_slot):
            masked = jnp.where(slot == of_slot, partial_value.astype(jnp.float32), 0.0)
            return modulation[of_slot, 2] * lax.psum_scatter(
                masked, "section", scatter_dimension=0, tiled=True
            )

        own_control = (own_control.astype(jnp.float32) + summed(2 * level)).astype(jnp.bfloat16)
        own_hidden = own_hidden.astype(jnp.float32) + summed(2 * level + 1)
        own_hidden = own_hidden + control_gain[level] * own_control.astype(jnp.float32)
        return own_hidden.astype(jnp.bfloat16), own_control

    own = embed(latent, control_latent, embed_weight, control_embed)
    own = lax.fori_loop(0, slot_count // 2, level_of, own)
    return jnp.dot(
        modulated(own[0], final_mod[0], final_mod[1]),
        final_weight,
        preferred_element_type=jnp.float32,
    )


def solution(mesh):
    return jax.shard_map(
        on_device,
        mesh=mesh,
        in_specs=(
            P(("grp", "section"), None),
            P(("grp", "section"), None),
            P(),
            P(),
            P(),
            P(),
            P(),
            P(),
            P(),
            P("section", None, None),
            P("section", None, None),
            P("section", "grp", None),
            P(),
            P(),
            P(),
        ),
        out_specs=P(("grp", "section"), None),
        check_vma=False,
    )
```

time: 693 us -> 97.1 us (0.14)
  waiting for transfers between devices: 351 us -> 4.71 us
  starting transfers between devices: 121 us -> 8.63 us
  matrix products: 75.3 us -> 0 us
  Pallas kernels: 0 us -> 74.5 us
  blocking collectives: 41.6 us -> 0 us
  other arithmetic: 37.4 us -> 1.97 us
  local copies, waits for them, and re-layouts: 38.4 us -> 6.73 us
  between operations: 13.5 us -> 0.2 us
  loops' own time: 13 us -> 0 us
    ppermute x40 -> x4, waiting for transfers between devices: 285 us -> 4.71 us  [gathered(): lax.ppermute(rows, 'section', [(i, i ^ step) for i in range(count)])]
    ppermute x40 -> x4, starting transfers between devices: 121 us -> 8.63 us  [gathered(): lax.ppermute(rows, 'section', [(i, i ^ step) for i in range(count)])]
    pallas_call x0 -> x2, Pallas kernels: none -> 74.5 us  [the longest x1 52.8 us: reduced(): pl.pallas_call(reduce_kernel, out_shape=jax.ShapeDtypeStruct((share, fina...]
    dot_general x31 -> x0, matrix products: 72.4 us -> none  [the longest x4 24.9 us: attend_group(): jnp.dot(modded, w_qkv, preferred_element_type=jnp.float32)]
    reduce_scatter x1 -> x0, waiting for transfers between devices: 65.8 us -> none  [on_device(): lax.psum_scatter(finished[3][:seq_rows], 'section', scatter_dimension=0,...]
    all_gather x2 -> x0, blocking collectives: 41.6 us -> none  [the longest x1 23.6 us: on_device(): lax.all_gather(latent, 'section', axis=0, tiled=True)]
    another operation x6 -> x0, loops' own time: 13 us -> none  [the longest x1 7.14 us: on_device(): finished = lax.fori_loop(0, slot_count + PATCHES - 1, run_tick, initial)]
    reduce_sum x22 -> x0, other arithmetic: 10.6 us -> none  [the longest x9 3.92 us: modulated(): centered = values - jnp.mean(values, axis=-1, keepdims=True)]
  transfers between devices with their start and end apart: 41 -> 4, of which waited for: 41 -> 3; matrix products, arithmetic and copies ran while one was open for 2% -> 3% of each run, Pallas kernels for 0% -> 0%
where the time goes in v1:
time: 97.1 us; the launch traced here: 96.7 us
  Pallas kernels  74.5 us (77%)
  starting transfers between devices  8.63 us (9%)
  local copies, waits for them, and re-layouts  6.73 us (7%)
  waiting for transfers between devices  4.71 us (5%)
  other arithmetic  1.97 us (2%)
    pallas_call x1, Pallas kernels, reduced(): pl.pallas_call(reduce_kernel, out_shape=jax.ShapeDtypeStruct((share, fina...  52.8 us
    pallas_call x1, Pallas kernels, attended_of(): pl.pallas_call(functools.partial(attend_kernel, len(sources) == 4), out_s...  21.6 us
    ppermute x4, starting transfers between devices, gathered(): lax.ppermute(rows, 'section', [(i, i ^ step) for i in range(count)])  8.63 us
    unnamed x28, local copies, waits for them, and re-layouts  6.73 us
    ppermute x4, waiting for transfers between devices, gathered(): lax.ppermute(rows, 'section', [(i, i ^ step) for i in range(count)])  4.71 us
  transfers between devices with their start and end apart: 4, of which 3 were waited for; matrix products, arithmetic and copies ran while one was open for 3% of the time, Pallas kernels for 0%

profile of v1, /device:TPU:0, one launch (start us, length us, event | category | flops | bytes accessed | tf_op | source)
XLA Modules:
  0.0 96.7 jit_solution(8945925220366322607)
XLA Ops:
  0.0 0.0 copy-start.6
  0.0 0.0 copy-start.5
  0.0 0.0 copy-start.4
  0.0 0.0 copy-start.9
  0.0 0.0 copy-start.10
  0.0 0.0 copy-start.11
  0.0 0.9 pad_maximum_fusion.4
  1.0 0.5 collective-permute-start
  1.4 0.8 collective-permute-done
  2.3 0.8 broadcast_select_fusion.7
  3.1 2.9 %collective-permute-start.1 = (bf16[96,128]{1,0:T(8,128)(2,1)S(1)}, bf16[96,128]{1,0:T(8,128)(2,1)S(1)}, u32[]{:S(2)}, u32[]{:S(2)}) collective-permute-start(bf16[96,128]{1,0:T(8,128)(2,1)S(1)} %pad_maximum_fusion.3), channel_id=1, source_target_pairs={{0,2},{1,3},{2,0},{3,1},{4,6},{5,7},{6,4},{7,5},{8,10},{9,11},{10,... | collective-permute-start | bytes 73736 | tf_op jit(solution)/shard_map/ppermute | solution.py:366
  6.0 1.8 %collective-permute-done.1 = bf16[96,128]{1,0:T(8,128)(2,1)S(1)} collective-permute-done((bf16[96,128]{1,0:T(8,128)(2,1)S(1)}, bf16[96,128]{1,0:T(8,128)(2,1)S(1)}, u32[]{:S(2)}, u32[]{:S(2)}) %collective-permute-start.1) | collective-permute-done | bytes 24608 | tf_op jit(solution)/shard_map/ppermute | solution.py:366
  7.8 2.1 %collective-permute-start.2 = (bf16[192,128]{1,0:T(8,128)(2,1)S(1)}, bf16[192,128]{1,0:T(8,128)(2,1)S(1)}, u32[]{:S(2)}, u32[]{:S(2)}) collective-permute-start(bf16[192,128]{1,0:T(8,128)(2,1)S(1)} %pad_maximum_fusion.2), channel_id=1, source_target_pairs={{0,4},{1,5},{2,6},{3,7},{4,0},{5,1},{6,2},{7,3},{8,12},{9,13},{10,... | collective-permute-start | bytes 147464 | tf_op jit(solution)/shard_map/ppermute | solution.py:366
  10.0 2.1 %collective-permute-done.2 = bf16[192,128]{1,0:T(8,128)(2,1)S(1)} collective-permute-done((bf16[192,128]{1,0:T(8,128)(2,1)S(1)}, bf16[192,128]{1,0:T(8,128)(2,1)S(1)}, u32[]{:S(2)}, u32[]{:S(2)}) %collective-permute-start.2) | collective-permute-done | bytes 49184 | tf_op jit(solution)/shard_map/ppermute | solution.py:366
  12.1 3.1 %collective-permute-start.3 = (bf16[384,128]{1,0:T(8,128)(2,1)S(1)}, bf16[384,128]{1,0:T(8,128)(2,1)S(1)}, u32[]{:S(2)}, u32[]{:S(2)}) collective-permute-start(bf16[384,128]{1,0:T(8,128)(2,1)S(1)} %pad_maximum_fusion.1), channel_id=1, source_target_pairs={{0,8},{1,9},{2,10},{3,11},{4,12},{5,13},{6,14},{7,15},{8,0},{9,1},... | collective-permute-start | bytes 294920 | tf_op jit(solution)/shard_map/ppermute | solution.py:366
  15.2 0.8 copy.16.tile_lists
  16.0 0.9 copy.17.modulation
  16.9 1.4 %copy.19.final_weight = bf16[3072,64]{1,0:T(8,128)(2,1)S(1)} copy(bf16[3072,64]{0,1:T(8,128)(2,1)} %param.29) | data formatting | bytes 786432 | tf_op args[14]
  18.3 0.0 collective-permute-done.3
  18.3 0.1 fusion
  18.5 0.0 copy-done.6
  18.5 0.0 copy-done.5
  18.5 0.0 copy-done.4
  18.5 0.0 copy-done.9
  18.5 0.0 copy-done.10
  18.5 0.0 copy-done.11
  18.5 0.0 copy-start.2
  18.5 3.0 %copy-done.2 = bf16[1,3072,1152]{2,1,0:T(8,128)(2,1)S(1)} copy-done((bf16[1,3072,1152]{2,1,0:T(8,128)(2,1)S(1)}, bf16[1,3072,1152]{2,1,0:T(8,128)(2,1)}, u32[]{:S(2)}) %copy-start.2) | copy-done | bytes 7077912
  21.5 0.0 copy-start
  21.5 0.0 copy-start.1
  21.5 0.0 copy-start.3
  21.6 0.0 copy-start.7
  21.6 0.0 copy-start.8
  21.6 21.6 %attend.1.attended = bf16[768,384]{1,0:T(8,128)(2,1)S(1)} custom-call(s32[4]{0:T(128)S(1)} %copy-done.11, s32[2,6,3]{2,1,0:T(8,128)S(1)} %copy.16.tile_lists, s32[2,6]{1,0:T(2,128)S(1)} %copy-done.10, f32[2,3,3072]{2,1,0:T(4,128)S(1)} %copy.17.modulation, f32[2,2,128]{2,1,0:T(2,128)S(1)} %copy-done.9, bf16[3072,1152]{1,0:T(8,128)(2,1)S(1)} %bitcast.3, ...), custom_call_target="tpu_custom_call" | custom-call | flops 6000000000 | bytes 10000000 | tf_op jit(solution)/shard_map/attend/pallas_call | solution.py:146
  43.2 0.0 copy-done
  43.2 0.0 copy-done.1
  43.2 0.0 copy-done.3
  43.2 0.0 copy-done.7
  43.3 0.0 copy-done.8
  43.3 52.8 %reduce_rows.1 = f32[48,64]{1,0:T(8,128)S(1)} custom-call(bf16[768,384]{1,0:T(8,128)(2,1)S(1)} %attend.1.attended, bf16[384,3072]{1,0:T(8,128)(2,1)S(1)} %bitcast.4, f32[2,3,3072]{2,1,0:T(4,128)S(1)} %copy.17.modulation, f32[1,3072]{1,0:T(1,128)S(1)} %copy-done.8, bf16[48,64]{1,0:T(8,128)(2,1)S(1)} %copy-done.1, bf16[48,64]{1,0:T(8,128)(2,1)S(1)} %copy-done, ...), custom_call_target="tpu_custom_call" | custom-call | flops 2000000000 | bytes 10000000 | tf_op jit(solution)/shard_map/reduce_rows/pallas_call | solution.py:323
  96.1 0.6 copy.21
  (6 shorter events, 0.1 us)
Async XLA Ops:
  0.0 18.5 %copy-start.6 = (bf16[64,3072]{1,0:T(8,128)(2,1)S(1)}, bf16[64,3072]{1,0:T(8,128)(2,1)}, u32[]{:S(2)}) copy-start(bf16[64,3072]{1,0:T(8,128)(2,1)} %control_embed.1) | copy-start | bytes 1179652
  0.0 18.5 %copy-start.5 = (bf16[64,3072]{1,0:T(8,128)(2,1)S(1)}, bf16[64,3072]{1,0:T(8,128)(2,1)}, u32[]{:S(2)}) copy-start(bf16[64,3072]{1,0:T(8,128)(2,1)} %embed_weight.1) | copy-start | bytes 1179652
  0.0 18.5 %copy-start.4 = (bf16[1,768,768]{2,1,0:T(8,128)(2,1)S(1)}, bf16[1,768,768]{2,1,0:T(8,128)(2,1)}, u32[]{:S(2)}) copy-start(bf16[1,768,768]{2,1,0:T(8,128)(2,1)} %param.26) | copy-start | bytes 3538948
  0.0 18.5 %copy-start.9 = (f32[2,2,128]{2,1,0:T(2,128)S(1)}, f32[2,2,128]{2,1,0:T(2,128)}, u32[]{:S(2)}) copy-start(f32[2,2,128]{2,1,0:T(2,128)} %qk_gain.1) | copy-start | bytes 6148
  0.0 18.5 %copy-start.10 = (s32[2,6]{1,0:T(2,128)S(1)}, s32[2,6]{1,0:T(2,128)}, u32[]{:S(2)}) copy-start(s32[2,6]{1,0:T(2,128)} %tile_counts.1) | copy-start | bytes 148
  0.0 18.5 %copy-start.11 = (s32[4]{0:T(128)S(1)}, s32[4]{0:T(128)}, u32[]{:S(2)}) copy-start(s32[4]{0:T(128)} %patch_tiles.1) | copy-start | bytes 52
  1.0 1.3 %collective-permute-start = (bf16[48,128]{1,0:T(8,128)(2,1)S(1)}, bf16[48,128]{1,0:T(8,128)(2,1)S(1)}, u32[]{:S(2)}, u32[]{:S(2)}) collective-permute-start(bf16[48,128]{1,0:T(8,128)(2,1)S(1)} %pad_maximum_fusion.4), channel_id=1, source_target_pairs={{0,1},{1,0},{2,3},{3,2},{4,5},{5,4},{6,7},{7,6},{8,9},{9,8},{10,11... | collective-permute-start | bytes 36872 | tf_op jit(solution)/shard_map/ppermute | solution.py:366
  3.1 4.7 %collective-permute-start.1 = (bf16[96,128]{1,0:T(8,128)(2,1)S(1)}, bf16[96,128]{1,0:T(8,128)(2,1)S(1)}, u32[]{:S(2)}, u32[]{:S(2)}) collective-permute-start(bf16[96,128]{1,0:T(8,128)(2,1)S(1)} %pad_maximum_fusion.3), channel_id=1, source_target_pairs={{0,2},{1,3},{2,0},{3,1},{4,6},{5,7},{6,4},{7,5},{8,10},{9,11},{10,... | collective-permute-start | bytes 73736 | tf_op jit(solution)/shard_map/ppermute | solution.py:366
  7.8 4.2 %collective-permute-start.2 = (bf16[192,128]{1,0:T(8,128)(2,1)S(1)}, bf16[192,128]{1,0:T(8,128)(2,1)S(1)}, u32[]{:S(2)}, u32[]{:S(2)}) collective-permute-start(bf16[192,128]{1,0:T(8,128)(2,1)S(1)} %pad_maximum_fusion.2), channel_id=1, source_target_pairs={{0,4},{1,5},{2,6},{3,7},{4,0},{5,1},{6,2},{7,3},{8,12},{9,13},{10,... | collective-permute-start | bytes 147464 | tf_op jit(solution)/shard_map/ppermute | solution.py:366
  12.1 6.2 %collective-permute-start.3 = (bf16[384,128]{1,0:T(8,128)(2,1)S(1)}, bf16[384,128]{1,0:T(8,128)(2,1)S(1)}, u32[]{:S(2)}, u32[]{:S(2)}) collective-permute-start(bf16[384,128]{1,0:T(8,128)(2,1)S(1)} %pad_maximum_fusion.1), channel_id=1, source_target_pairs={{0,8},{1,9},{2,10},{3,11},{4,12},{5,13},{6,14},{7,15},{8,0},{9,1},... | collective-permute-start | bytes 294920 | tf_op jit(solution)/shard_map/ppermute | solution.py:366
  18.5 3.0 %copy-start.2 = (bf16[1,3072,1152]{2,1,0:T(8,128)(2,1)S(1)}, bf16[1,3072,1152]{2,1,0:T(8,128)(2,1)}, u32[]{:S(2)}) copy-start(bf16[1,3072,1152]{2,1,0:T(8,128)(2,1)} %param.24) | copy-start | bytes 21233668
  21.5 21.7 %copy-start = (bf16[48,64]{1,0:T(8,128)(2,1)S(1)}, bf16[48,64]{1,0:T(8,128)(2,1)}, u32[]{:S(2)}) copy-start(bf16[48,64]{1,0:T(8,128)(2,1)} %control_latent.1) | copy-start | bytes 18436
  21.5 21.7 %copy-start.1 = (bf16[48,64]{1,0:T(8,128)(2,1)S(1)}, bf16[48,64]{1,0:T(8,128)(2,1)}, u32[]{:S(2)}) copy-start(bf16[48,64]{1,0:T(8,128)(2,1)} %latent.1) | copy-start | bytes 18436
  21.5 21.7 %copy-start.3 = (bf16[1,384,3072]{2,1,0:T(8,128)(2,1)S(1)}, bf16[1,384,3072]{2,1,0:T(8,128)(2,1)}, u32[]{:S(2)}) copy-start(bf16[1,384,3072]{2,1,0:T(8,128)(2,1)} %param.25) | copy-start | bytes 7077892
  21.6 21.7 %copy-start.7 = (f32[2,3072]{1,0:T(2,128)S(1)}, f32[2,3072]{1,0:T(2,128)}, u32[]{:S(2)}) copy-start(f32[2,3072]{1,0:T(2,128)} %tail.1) | copy-start | bytes 73732
  21.6 21.7 %copy-start.8 = (f32[1,3072]{1,0:T(1,128)S(1)}, f32[1,3072]{1,0:T(1,128)}, u32[]{:S(2)}) copy-start(f32[1,3072]{1,0:T(1,128)} %control_gain.1) | copy-start | bytes 36868

commit v2 on v1

--- a/solution.py
+++ b/solution.py
@@ -12,8 +12,8 @@
 HG = 8
 TILE = 128
 EPSILON = 1e-06
-CHUNKS = 6
-Y_FIRST = (True, True, False, True, True, False)
+CHUNKS = 8
+Y_FIRST = (True, True, False, True, True, False, True, True)
 MESH = pl.DeviceIdType.MESH
 
 

time: 97.1 us -> 101 us (1.040)
  Pallas kernels: 74.5 us -> 78.2 us
    pallas_call x1, Pallas kernels: 52.8 us -> 56.6 us  [reduced(): pl.pallas_call(reduce_kernel, out_shape=jax.ShapeDtypeStruct((share, fina...]
where the time goes in v2:
time: 101 us; the launch traced here: 100 us
  Pallas kernels  78.2 us (77%)
  starting transfers between devices  8.63 us (9%)
  local copies, waits for them, and re-layouts  6.73 us (7%)
  waiting for transfers between devices  4.71 us (5%)
  other arithmetic  1.97 us (2%)
    pallas_call x1, Pallas kernels, reduced(): pl.pallas_call(reduce_kernel, out_shape=jax.ShapeDtypeStruct((share, fina...  56.6 us
    pallas_call x1, Pallas kernels, attended_of(): pl.pallas_call(functools.partial(attend_kernel, len(sources) == 4), out_s...  21.6 us
    ppermute x4, starting transfers between devices, gathered(): lax.ppermute(rows, 'section', [(i, i ^ step) for i in range(count)])  8.63 us
    unnamed x28, local copies, waits for them, and re-layouts  6.73 us
    ppermute x4, waiting for transfers between devices, gathered(): lax.ppermute(rows, 'section', [(i, i ^ step) for i in range(count)])  4.71 us
  transfers between devices with their start and end apart: 4, of which 3 were waited for; matrix products, arithmetic and copies ran while one was open for 3% of the time, Pallas kernels for 0%

profile of v2, /device:TPU:0, one launch (start us, length us, event | category | flops | bytes accessed | tf_op | source)
XLA Modules:
  0.0 100.5 jit_solution(17381809177452485014)
XLA Ops:
  0.0 0.0 copy-start.6
  0.0 0.0 copy-start.5
  0.0 0.0 copy-start.4
  0.0 0.0 copy-start.9
  0.0 0.0 copy-start.10
  0.0 0.0 copy-start.11
  0.0 0.9 pad_maximum_fusion.4
  1.0 0.5 collective-permute-start
  1.4 0.8 collective-permute-done
  2.3 0.8 broadcast_select_fusion.7
  3.1 2.9 %collective-permute-start.1 = (bf16[96,128]{1,0:T(8,128)(2,1)S(1)}, bf16[96,128]{1,0:T(8,128)(2,1)S(1)}, u32[]{:S(2)}, u32[]{:S(2)}) collective-permute-start(bf16[96,128]{1,0:T(8,128)(2,1)S(1)} %pad_maximum_fusion.3), channel_id=1, source_target_pairs={{0,2},{1,3},{2,0},{3,1},{4,6},{5,7},{6,4},{7,5},{8,10},{9,11},{10,... | collective-permute-start | bytes 73736 | tf_op jit(solution)/shard_map/ppermute | solution.py:366
  6.0 1.8 %collective-permute-done.1 = bf16[96,128]{1,0:T(8,128)(2,1)S(1)} collective-permute-done((bf16[96,128]{1,0:T(8,128)(2,1)S(1)}, bf16[96,128]{1,0:T(8,128)(2,1)S(1)}, u32[]{:S(2)}, u32[]{:S(2)}) %collective-permute-start.1) | collective-permute-done | bytes 24608 | tf_op jit(solution)/shard_map/ppermute | solution.py:366
  7.8 2.1 %collective-permute-start.2 = (bf16[192,128]{1,0:T(8,128)(2,1)S(1)}, bf16[192,128]{1,0:T(8,128)(2,1)S(1)}, u32[]{:S(2)}, u32[]{:S(2)}) collective-permute-start(bf16[192,128]{1,0:T(8,128)(2,1)S(1)} %pad_maximum_fusion.2), channel_id=1, source_target_pairs={{0,4},{1,5},{2,6},{3,7},{4,0},{5,1},{6,2},{7,3},{8,12},{9,13},{10,... | collective-permute-start | bytes 147464 | tf_op jit(solution)/shard_map/ppermute | solution.py:366
  10.0 2.1 %collective-permute-done.2 = bf16[192,128]{1,0:T(8,128)(2,1)S(1)} collective-permute-done((bf16[192,128]{1,0:T(8,128)(2,1)S(1)}, bf16[192,128]{1,0:T(8,128)(2,1)S(1)}, u32[]{:S(2)}, u32[]{:S(2)}) %collective-permute-start.2) | collective-permute-done | bytes 49184 | tf_op jit(solution)/shard_map/ppermute | solution.py:366
  12.1 3.1 %collective-permute-start.3 = (bf16[384,128]{1,0:T(8,128)(2,1)S(1)}, bf16[384,128]{1,0:T(8,128)(2,1)S(1)}, u32[]{:S(2)}, u32[]{:S(2)}) collective-permute-start(bf16[384,128]{1,0:T(8,128)(2,1)S(1)} %pad_maximum_fusion.1), channel_id=1, source_target_pairs={{0,8},{1,9},{2,10},{3,11},{4,12},{5,13},{6,14},{7,15},{8,0},{9,1},... | collective-permute-start | bytes 294920 | tf_op jit(solution)/shard_map/ppermute | solution.py:366
  15.2 0.8 copy.16.tile_lists
  16.0 0.9 copy.17.modulation
  16.9 1.4 %copy.19.final_weight = bf16[3072,64]{1,0:T(8,128)(2,1)S(1)} copy(bf16[3072,64]{0,1:T(8,128)(2,1)} %param.29) | data formatting | bytes 786432 | tf_op args[14]
  18.3 0.0 collective-permute-done.3
  18.3 0.1 fusion
  18.5 0.0 copy-done.6
  18.5 0.0 copy-done.5
  18.5 0.0 copy-done.4
  18.5 0.0 copy-done.9
  18.5 0.0 copy-done.10
  18.5 0.0 copy-done.11
  18.5 0.0 copy-start.2
  18.5 3.0 %copy-done.2 = bf16[1,3072,1152]{2,1,0:T(8,128)(2,1)S(1)} copy-done((bf16[1,3072,1152]{2,1,0:T(8,128)(2,1)S(1)}, bf16[1,3072,1152]{2,1,0:T(8,128)(2,1)}, u32[]{:S(2)}) %copy-start.2) | copy-done | bytes 7077912
  21.5 0.0 copy-start
  21.5 0.0 copy-start.1
  21.5 0.0 copy-start.3
  21.6 0.0 copy-start.7
  21.6 0.0 copy-start.8
  21.6 21.6 %attend.1.attended = bf16[768,384]{1,0:T(8,128)(2,1)S(1)} custom-call(s32[4]{0:T(128)S(1)} %copy-done.11, s32[2,6,3]{2,1,0:T(8,128)S(1)} %copy.16.tile_lists, s32[2,6]{1,0:T(2,128)S(1)} %copy-done.10, f32[2,3,3072]{2,1,0:T(4,128)S(1)} %copy.17.modulation, f32[2,2,128]{2,1,0:T(2,128)S(1)} %copy-done.9, bf16[3072,1152]{1,0:T(8,128)(2,1)S(1)} %bitcast.3, ...), custom_call_target="tpu_custom_call" | custom-call | flops 6000000000 | bytes 10000000 | tf_op jit(solution)/shard_map/attend/pallas_call | solution.py:146
  43.2 0.0 copy-done
  43.2 0.0 copy-done.1
  43.2 0.0 copy-done.3
  43.2 0.0 copy-done.7
  43.3 0.0 copy-done.8
  43.3 56.6 %reduce_rows.1 = f32[48,64]{1,0:T(8,128)S(1)} custom-call(bf16[768,384]{1,0:T(8,128)(2,1)S(1)} %attend.1.attended, bf16[384,3072]{1,0:T(8,128)(2,1)S(1)} %bitcast.4, f32[2,3,3072]{2,1,0:T(4,128)S(1)} %copy.17.modulation, f32[1,3072]{1,0:T(1,128)S(1)} %copy-done.8, bf16[48,64]{1,0:T(8,128)(2,1)S(1)} %copy-done.1, bf16[48,64]{1,0:T(8,128)(2,1)S(1)} %copy-done, ...), custom_call_target="tpu_custom_call" | custom-call | flops 2000000000 | bytes 10000000 | tf_op jit(solution)/shard_map/reduce_rows/pallas_call | solution.py:323
  99.9 0.6 copy.21
  (6 shorter events, 0.1 us)
Async XLA Ops:
  0.0 18.5 %copy-start.6 = (bf16[64,3072]{1,0:T(8,128)(2,1)S(1)}, bf16[64,3072]{1,0:T(8,128)(2,1)}, u32[]{:S(2)}) copy-start(bf16[64,3072]{1,0:T(8,128)(2,1)} %control_embed.1) | copy-start | bytes 1179652
  0.0 18.5 %copy-start.5 = (bf16[64,3072]{1,0:T(8,128)(2,1)S(1)}, bf16[64,3072]{1,0:T(8,128)(2,1)}, u32[]{:S(2)}) copy-start(bf16[64,3072]{1,0:T(8,128)(2,1)} %embed_weight.1) | copy-start | bytes 1179652
  0.0 18.5 %copy-start.4 = (bf16[1,768,768]{2,1,0:T(8,128)(2,1)S(1)}, bf16[1,768,768]{2,1,0:T(8,128)(2,1)}, u32[]{:S(2)}) copy-start(bf16[1,768,768]{2,1,0:T(8,128)(2,1)} %param.26) | copy-start | bytes 3538948
  0.0 18.5 %copy-start.9 = (f32[2,2,128]{2,1,0:T(2,128)S(1)}, f32[2,2,128]{2,1,0:T(2,128)}, u32[]{:S(2)}) copy-start(f32[2,2,128]{2,1,0:T(2,128)} %qk_gain.1) | copy-start | bytes 6148
  0.0 18.5 %copy-start.10 = (s32[2,6]{1,0:T(2,128)S(1)}, s32[2,6]{1,0:T(2,128)}, u32[]{:S(2)}) copy-start(s32[2,6]{1,0:T(2,128)} %tile_counts.1) | copy-start | bytes 148
  0.0 18.5 %copy-start.11 = (s32[4]{0:T(128)S(1)}, s32[4]{0:T(128)}, u32[]{:S(2)}) copy-start(s32[4]{0:T(128)} %patch_tiles.1) | copy-start | bytes 52
  1.0 1.3 %collective-permute-start = (bf16[48,128]{1,0:T(8,128)(2,1)S(1)}, bf16[48,128]{1,0:T(8,128)(2,1)S(1)}, u32[]{:S(2)}, u32[]{:S(2)}) collective-permute-start(bf16[48,128]{1,0:T(8,128)(2,1)S(1)} %pad_maximum_fusion.4), channel_id=1, source_target_pairs={{0,1},{1,0},{2,3},{3,2},{4,5},{5,4},{6,7},{7,6},{8,9},{9,8},{10,11... | collective-permute-start | bytes 36872 | tf_op jit(solution)/shard_map/ppermute | solution.py:366
  3.1 4.7 %collective-permute-start.1 = (bf16[96,128]{1,0:T(8,128)(2,1)S(1)}, bf16[96,128]{1,0:T(8,128)(2,1)S(1)}, u32[]{:S(2)}, u32[]{:S(2)}) collective-permute-start(bf16[96,128]{1,0:T(8,128)(2,1)S(1)} %pad_maximum_fusion.3), channel_id=1, source_target_pairs={{0,2},{1,3},{2,0},{3,1},{4,6},{5,7},{6,4},{7,5},{8,10},{9,11},{10,... | collective-permute-start | bytes 73736 | tf_op jit(solution)/shard_map/ppermute | solution.py:366
  7.8 4.2 %collective-permute-start.2 = (bf16[192,128]{1,0:T(8,128)(2,1)S(1)}, bf16[192,128]{1,0:T(8,128)(2,1)S(1)}, u32[]{:S(2)}, u32[]{:S(2)}) collective-permute-start(bf16[192,128]{1,0:T(8,128)(2,1)S(1)} %pad_maximum_fusion.2), channel_id=1, source_target_pairs={{0,4},{1,5},{2,6},{3,7},{4,0},{5,1},{6,2},{7,3},{8,12},{9,13},{10,... | collective-permute-start | bytes 147464 | tf_op jit(solution)/shard_map/ppermute | solution.py:366
  12.1 6.2 %collective-permute-start.3 = (bf16[384,128]{1,0:T(8,128)(2,1)S(1)}, bf16[384,128]{1,0:T(8,128)(2,1)S(1)}, u32[]{:S(2)}, u32[]{:S(2)}) collective-permute-start(bf16[384,128]{1,0:T(8,128)(2,1)S(1)} %pad_maximum_fusion.1), channel_id=1, source_target_pairs={{0,8},{1,9},{2,10},{3,11},{4,12},{5,13},{6,14},{7,15},{8,0},{9,1},... | collective-permute-start | bytes 294920 | tf_op jit(solution)/shard_map/ppermute | solution.py:366
  18.5 3.0 %copy-start.2 = (bf16[1,3072,1152]{2,1,0:T(8,128)(2,1)S(1)}, bf16[1,3072,1152]{2,1,0:T(8,128)(2,1)}, u32[]{:S(2)}) copy-start(bf16[1,3072,1152]{2,1,0:T(8,128)(2,1)} %param.24) | copy-start | bytes 21233668
  21.5 21.7 %copy-start = (bf16[48,64]{1,0:T(8,128)(2,1)S(1)}, bf16[48,64]{1,0:T(8,128)(2,1)}, u32[]{:S(2)}) copy-start(bf16[48,64]{1,0:T(8,128)(2,1)} %control_latent.1) | copy-start | bytes 18436
  21.5 21.7 %copy-start.1 = (bf16[48,64]{1,0:T(8,128)(2,1)S(1)}, bf16[48,64]{1,0:T(8,128)(2,1)}, u32[]{:S(2)}) copy-start(bf16[48,64]{1,0:T(8,128)(2,1)} %latent.1) | copy-start | bytes 18436
  21.5 21.7 %copy-start.3 = (bf16[1,384,3072]{2,1,0:T(8,128)(2,1)S(1)}, bf16[1,384,3072]{2,1,0:T(8,128)(2,1)}, u32[]{:S(2)}) copy-start(bf16[1,384,3072]{2,1,0:T(8,128)(2,1)} %param.25) | copy-start | bytes 7077892
  21.6 21.7 %copy-start.7 = (f32[2,3072]{1,0:T(2,128)S(1)}, f32[2,3072]{1,0:T(2,128)}, u32[]{:S(2)}) copy-start(f32[2,3072]{1,0:T(2,128)} %tail.1) | copy-start | bytes 73732
  21.6 21.7 %copy-start.8 = (f32[1,3072]{1,0:T(1,128)S(1)}, f32[1,3072]{1,0:T(1,128)}, u32[]{:S(2)}) copy-start(f32[1,3072]{1,0:T(1,128)} %control_gain.1) | copy-start | bytes 36868
